TPU v7x, 512 devices: a whole 4x8x8 slice. The times are simulated.
512 devices in a mesh: leaf: 32 (over y, x), front: 16 (over z, core).
Axes of the slice: x: 4, y: 8, z: 8, core: 2. Of those that a mesh axis runs over, the one named last changes fastest.
Arguments:
- root_inverse: bfloat16 [384, 384], P('front')
- root_rhs: bfloat16 [384, 256], P('front'), may hold values from -6 to 6
- mid_panels: bfloat16 [4, 384, 384], P(None, 'front'), may hold values from -0.3125 to 0.3125
- mid_rows: int32 [4, 384], replicated, may hold values from 0 to 383, as said below
- mid_inverse: bfloat16 [4, 384, 384], P(None, 'front')
- mid_rhs: bfloat16 [4, 384, 256], P(None, 'front'), may hold values from -6 to 6
- parent_list: int32 [1024, 1], replicated, may hold values from 0 to 3
- sub_panels: bfloat16 [1024, 384, 384], P(('leaf', 'front')), may hold values from -0.3125 to 0.3125
- sub_rows: int32 [1024, 384], P(('leaf', 'front')), may hold values from 0 to 767, as said below
- sub_inverse: bfloat16 [1024, 384, 384], P(('leaf', 'front'))
- sub_rhs: bfloat16 [1024, 384, 256], P(('leaf', 'front')), may hold values from -6 to 6
- group_of: int32 [1024], P(('leaf', 'front')), may hold values from 0 to 1023, as said below
- leaf_panels: bfloat16 [1024, 384, 384], P(('leaf', 'front')), may hold values from -0.3125 to 0.3125
- leaf_rows: int32 [1024, 384], P(('leaf', 'front')), may hold values from 0 to 1151, as said below
- leaf_inverse: bfloat16 [1024, 384, 384], P(('leaf', 'front'))
- leaf_rhs: bfloat16 [1024, 384, 256], P(('leaf', 'front')), may hold values from -6 to 6
- live_cols: int32 [1024], P(('leaf', 'front')), may hold values from 192 to 384
Outputs:
- root_solution: bfloat16 [384, 256], P('front')
- mid_solution: bfloat16 [4, 384, 256], P(None, 'front')
- sub_solution: bfloat16 [1024, 384, 256], P(('leaf', 'front'))
- leaf_solution: bfloat16 [1024, 384, 256], P(('leaf', 'front'))
Inputs may be any that keep to these rules, and one draw needn't show every extreme that they name: `mid_rows`: each row lists 384 different unknowns of the root. `sub_rows`: each row lists 384 different numbers; a < 384 names the root's unknown a, otherwise unknown a - 384 of the level-1 parent. `leaf_rows`: each row lists 384 different numbers; a < 384 names the root's unknown a, a < 768 unknown a - 384 of the level-1 grandparent, otherwise unknown a - 768 of the level-2 parent. `parent_list`: every level-1 supernode is the parent of some level-2 supernode. `group_of`: level-3 supernodes come in blocks of 2 and level-2 supernodes in blocks of 2, both numbered 0 to 511; the parent of a supernode of block d lies in a block whose cyclic distance from d is at most 2, and that distance is reached.
All inputs are finite; a program needn't handle non-finite values.
Results may differ from a plain program's by a relative error of at most 0.0067.
Values may be sent and summed in bfloat16 or wider, within the bound.
No kernel may reach another device: no remote copies, remote signals or barrier semaphores. Data moves between devices by JAX's collectives and lax.ppermute only.
A program may use at most 64 MiB of HBM per device.

v0:
```python
import jax
import jax.numpy as jnp
from jax import lax
from jax.sharding import PartitionSpec as P

HOP = 2


def from_behind(block, axis, distance):
    devices = range(lax.axis_size(axis))
    route = [((i - distance) % len(devices), i) for i in devices]
    return lax.ppermute(block, axis, route)


def pick_rows(known_rows, row_index):
    picked = jnp.take(known_rows, row_index.reshape(-1), axis=0)
    return picked.reshape(row_index.shape + (known_rows.shape[1],))


def local_update(panels, picked, rhs_rows):
    products = jnp.einsum("nrw,nrk->nwk", panels, picked, preferred_element_type=jnp.float32)
    return (rhs_rows.astype(jnp.float32) - products).astype(jnp.bfloat16)


def inverse_apply(inverse_rows, update):
    return jnp.einsum("nji,nik->njk", inverse_rows, update, preferred_element_type=jnp.float32)


def spread_solved(own_rows):
    return lax.all_gather(own_rows, "front", axis=1, tiled=True)


def per_device(
    root_inverse,
    root_rhs,
    mid_panels,
    mid_rows,
    mid_inverse,
    mid_rhs,
    parent_list,
    sub_panels,
    sub_rows,
    sub_inverse,
    sub_rhs,
    group_of,
    leaf_panels,
    leaf_rows,
    leaf_inverse,
    leaf_rhs,
    live_cols,
):
    block_width = root_inverse.shape[1]
    rhs_count = root_rhs.shape[1]
    row_count = root_inverse.shape[0]
    front_at = lax.axis_index("front")
    first_row = front_at * row_count
    rhs_whole = lax.all_gather(root_rhs, "front", axis=0, tiled=True)
    root_own = jnp.dot(root_inverse, rhs_whole, preferred_element_type=jnp.float32).astype(
        jnp.bfloat16
    )
    root_known = spread_solved(root_own[None])[0]
    panel_count = mid_panels.shape[1]
    own_index = lax.dynamic_slice_in_dim(mid_rows, front_at * panel_count, panel_count, 1)
    mid_picked = pick_rows(root_known, own_index)
    products = jnp.einsum(
        "nrw,nrk->nwk", mid_panels, mid_picked, preferred_element_type=jnp.float32
    )
    own_part = lax.dynamic_slice_in_dim(products, first_row, row_count, 1)
    partials = lax.dynamic_update_slice_in_dim(
        -products, mid_rhs.astype(jnp.float32) - own_part, first_row, 1
    )
    mid_update = lax.psum(partials, "front").astype(jnp.bfloat16)
    mid_own = inverse_apply(mid_inverse, mid_update).astype(jnp.bfloat16)
    mid_whole = spread_solved(mid_own)
    mid_count = mid_whole.shape[0]
    sub_count = sub_panels.shape[0]
    here = lax.axis_index(("leaf", "front"))
    parent_column = parent_list[:, 0]
    parents = lax.dynamic_slice_in_dim(parent_column, here * sub_count, sub_count)
    known_rows = jnp.concatenate([root_known, mid_whole.reshape(-1, rhs_count)], axis=0)
    sub_index = jnp.where(
        sub_rows < block_width, sub_rows, parents[:, None] * block_width + sub_rows
    )
    sub_picked = pick_rows(known_rows, sub_index)
    sub_solution = inverse_apply(sub_inverse, local_update(sub_panels, sub_picked, sub_rhs)).astype(
        jnp.bfloat16
    )
    nearby = []
    for offset in range(-HOP, HOP + 1):
        if offset == 0:
            nearby.append(sub_solution)
        else:
            nearby.append(from_behind(sub_solution, ("leaf", "front"), -offset))
    sources = jnp.concatenate(nearby, axis=0)
    block_total = lax.axis_size(("leaf", "front"))
    owner_block = group_of // sub_count
    distance = (owner_block - here + block_total + HOP) % block_total
    source_slot = distance * sub_count + group_of % sub_count
    matches = group_of[:, None] == jnp.arange(parent_column.shape[0], dtype=jnp.int32)[None, :]
    grandparent = jnp.sum(jnp.where(matches, parent_column[None, :], 0), axis=1)
    all_known = jnp.concatenate([known_rows, sources.reshape(-1, rhs_count)], axis=0)
    leaf_index = jnp.where(
        leaf_rows < block_width,
        leaf_rows,
        jnp.where(
            leaf_rows < 2 * block_width,
            grandparent[:, None] * block_width + leaf_rows,
            (mid_count - 1 + source_slot[:, None]) * block_width + leaf_rows,
        ),
    )
    leaf_picked = pick_rows(all_known, leaf_index)
    solved = inverse_apply(leaf_inverse, local_update(leaf_panels, leaf_picked, leaf_rhs))
    live_mask = jnp.arange(block_width, dtype=jnp.int32)[None, :] < live_cols[:, None]
    leaf_solution = jnp.where(live_mask[:, :, None], solved, jnp.float32(0.0)).astype(jnp.bfloat16)
    return (root_own, mid_own, sub_solution, leaf_solution)


def solution(mesh):
    return jax.shard_map(
        per_device,
        mesh=mesh,
        in_specs=(
            P("front", None),
            P("front", None),
            P(None, "front", None),
            P(),
            P(None, "front", None),
            P(None, "front", None),
            P(),
            P(("leaf", "front"), None, None),
            P(("leaf", "front"), None),
            P(("leaf", "front"), None, None),
            P(("leaf", "front"), None, None),
            P(("leaf", "front")),
            P(("leaf", "front"), None, None),
            P(("leaf", "front"), None),
            P(("leaf", "front"), None, None),
            P(("leaf", "front"), None, None),
            P(("leaf", "front")),
        ),
        out_specs=(
            P("front", None),
            P(None, "front", None),
            P(("leaf", "front"), None, None),
            P(("leaf", "front"), None, None),
        ),
        check_vma=False,
    )
```

profile of v0, /device:TPU:1, one launch (start us, length us, event | category | flops | bytes accessed | tf_op | source)
XLA Modules:
  0.0 167.1 jit_solution(11506394017786851539)
XLA Ops:
  0.6 0.0 copy-start
  0.7 0.8 compare_and_fusion.2
  1.5 0.1 reshape.177
  1.6 25.3 %all_gather.9 = bf16[384,256]{1,0:T(8,128)(2,1)S(1)} all-gather(bf16[24,256]{1,0:T(8,128)(2,1)} %param.18), channel_id=1, replica_groups=mesh['leaf'=32,'front'=16] {'front'}, dimensions={0}, use_global_device_ids=true | all-gather | bytes 208896 | tf_op jit(solution)/shard_map/all_gather | solution.py:57
  26.8 0.9 convolution_convert_fusion.2
  27.7 0.0 copy-start.7
  27.7 15.0 %all-gather = bf16[384,256]{1,0:T(8,128)(2,1)S(1)} all-gather(bf16[24,256]{1,0:T(8,128)(2,1)S(1)} %convolution_convert_fusion.2), channel_id=2, replica_groups=mesh['leaf'=32,'front'=16] {'front'}, dimensions={0}, use_global_device_ids=true | all-gather | bytes 208896 | tf_op jit(solution)/shard_map/all_gather | solution.py:30
  42.7 0.8 gather_fusion
  43.5 1.4 fusion.23
  44.9 0.2 constant_dynamic-slice_fusion.1
  45.1 0.1 negate_bitcast_fusion
  45.3 0.3 copy-done.10
  45.6 0.1 fusion.32
  45.7 0.1 fusion.41
  45.7 0.1 compare_and_fusion.1
  45.8 0.2 copy.54
  46.0 0.2 copy.44
  46.2 3.3 %dynamic_update_slice.3 = f32[4,384,256]{1,2,0:T(8,128)S(1)} dynamic-update-slice(f32[4,384,256]{1,2,0:T(8,128)S(1)} %negate_bitcast_fusion, f32[4,24,256]{1,2,0:T(8,128)S(1)} %copy.44, s32[]{:T(128)} %constant.87.clone.1, s32[]{:T(128)S(6)} %select_n.108, s32[]{:T(128)} %constant.87.clone.1) | dynamic-update-slice | bytes 196612 | tf_op jit(solution)/shard_map/dynamic_update_slice | solution.py:69
  49.5 54.5 %all-reduce.1 = bf16[4,384,256]{1,2,0:T(8,128)(2,1)S(1)} all-reduce(f32[4,384,256]{1,2,0:T(8,128)S(1)} %dynamic_update_slice.3), channel_id=1, replica_groups=mesh['leaf'=32,'front'=16] {'front'}, use_global_device_ids=true, to_apply=%region_0.1 | all-reduce | flops 393216 | bytes 2359296 | tf_op jit(solution)/shard_map/psum | solution.py:72
  104.1 0.4 fusion.7
  104.5 20.2 %all_gather.11 = bf16[4,384,256]{2,1,0:T(8,128)(2,1)S(1)} all-gather(bf16[4,24,256]{2,1,0:T(8,128)(2,1)S(1)} %fusion.7), channel_id=1, replica_groups=mesh['leaf'=32,'front'=16] {'front'}, dimensions={1}, use_global_device_ids=true | all-gather | bytes 835584 | tf_op jit(solution)/shard_map/all_gather | solution.py:30
  124.7 0.9 copy-done.1
  125.6 0.1 pad_maximum_fusion.1
  125.7 0.2 fusion.27
  125.9 0.1 compare_and_fusion
  126.1 2.7 %gather_fusion.1 = bf16[768,256]{1,0:T(8,128)(2,1)S(1)} fusion(bf16[1920,256]{1,0:T(8,128)(2,1)S(1)} %pad_maximum_fusion.1, s32[1024]{0:T(1024)S(1)} %get-tuple-element.25), kind=kCustom, calls=%fused_computation.1 | custom fusion | bytes 789504 | tf_op jit(solution)/shard_map/jit(_take)/gather | solution.py:16
  128.8 0.2 copy.47
  129.0 0.2 copy.46
  129.2 0.6 fusion.6
  129.9 3.3 %collective-permute-start = (bf16[2,384,256]{1,2,0:T(8,128)(2,1)S(1)}, bf16[2,384,256]{1,2,0:T(8,128)(2,1)}, u32[]{:S(2)}, u32[]{:S(2)}) collective-permute-start(bf16[2,384,256]{1,2,0:T(8,128)(2,1)S(1)} %fusion.6), channel_id=1, source_target_pairs={{510,0},{511,1},{0,2},{1,3},{2,4},{3,5},{4,6},{5,7},{6,8},{7,9},{8... | collective-permute-start | bytes 1179656 | tf_op jit(solution)/shard_map/ppermute | solution.py:12
  133.2 2.0 %collective-permute-start.1 = (bf16[2,384,256]{1,2,0:T(8,128)(2,1)S(1)}, bf16[2,384,256]{1,2,0:T(8,128)(2,1)}, u32[]{:S(2)}, u32[]{:S(2)}) collective-permute-start(bf16[2,384,256]{1,2,0:T(8,128)(2,1)S(1)} %fusion.6), channel_id=1, source_target_pairs={{511,0},{0,1},{1,2},{2,3},{3,4},{4,5},{5,6},{6,7},{7,8},{8,9},{9,1... | collective-permute-start | bytes 1179656 | tf_op jit(solution)/shard_map/ppermute | solution.py:12
  135.2 2.4 %collective-permute-start.2 = (bf16[2,384,256]{1,2,0:T(8,128)(2,1)S(1)}, bf16[2,384,256]{1,2,0:T(8,128)(2,1)}, u32[]{:S(2)}, u32[]{:S(2)}) collective-permute-start(bf16[2,384,256]{1,2,0:T(8,128)(2,1)S(1)} %fusion.6), channel_id=1, source_target_pairs={{1,0},{2,1},{3,2},{4,3},{5,4},{6,5},{7,6},{8,7},{9,8},{10,9},{11,1... | collective-permute-start | bytes 1179656 | tf_op jit(solution)/shard_map/ppermute | solution.py:12
  137.6 8.6 %collective-permute-start.3 = (bf16[2,384,256]{1,2,0:T(8,128)(2,1)S(1)}, bf16[2,384,256]{1,2,0:T(8,128)(2,1)S(1)}, u32[]{:S(2)}, u32[]{:S(2)}) collective-permute-start(bf16[2,384,256]{1,2,0:T(8,128)(2,1)S(1)} %fusion.6), channel_id=1, source_target_pairs={{2,0},{3,1},{4,2},{5,3},{6,4},{7,5},{8,6},{9,7},{10,8},{11,9},{12,... | collective-permute-start | bytes 1179656 | tf_op jit(solution)/shard_map/ppermute | solution.py:12
  146.2 0.1 iota_compare_fusion
  146.3 0.9 copy.51
  147.2 0.9 copy.48
  148.1 1.0 constant_dynamic-update-slice_fusion.4
  149.2 1.1 constant_dynamic-update-slice_fusion.3
  150.2 0.1 constant_dynamic-update-slice_fusion.2
  150.3 1.1 constant_dynamic-update-slice_fusion.1
  151.4 3.8 %collective-permute-done.3 = bf16[2,384,256]{1,2,0:T(8,128)(2,1)S(1)} collective-permute-done((bf16[2,384,256]{1,2,0:T(8,128)(2,1)S(1)}, bf16[2,384,256]{1,2,0:T(8,128)(2,1)S(1)}, u32[]{:S(2)}, u32[]{:S(2)}) %collective-permute-start.3) | collective-permute-done | bytes 393248 | tf_op jit(solution)/shard_map/ppermute | solution.py:12
  155.1 0.1 constant_dynamic-update-slice_fusion
  155.2 2.5 %copy.49 = bf16[10,384,256]{2,1,0:T(8,128)(2,1)} copy(bf16[10,384,256]{1,2,0:T(8,128)(2,1)S(1)} %constant_dynamic-update-slice_fusion) | data formatting | bytes 3932160 | tf_op jit(solution)/shard_map/concatenate | solution.py:94
  157.7 1.9 %pad_maximum_fusion = bf16[5760,256]{1,0:T(8,128)(2,1)S(1)} fusion(bf16[3840,256]{1,0:T(8,128)(2,1)} %bitcast.56, bf16[1536,256]{1,0:T(8,128)(2,1)} %bitcast.58, bf16[384,256]{1,0:T(8,128)(2,1)} %copy-done.2), kind=kLoop, calls=%fused_computation.3 | loop fusion | flops 8847360 | bytes 5898240 | tf_op jit(solution)/shard_map/concatenate | solution.py:101
  159.7 3.3 %gather_fusion.2 = bf16[768,256]{1,0:T(8,128)(2,1)} fusion(bf16[5760,256]{1,0:T(8,128)(2,1)S(1)} %pad_maximum_fusion, s32[1024]{0:T(1024)S(1)} %get-tuple-element.24), kind=kCustom, calls=%fused_computation.2 | custom fusion | bytes 789504 | tf_op jit(solution)/shard_map/jit(_take)/gather | solution.py:16
  162.9 1.2 copy.50
  164.1 2.0 %fusion.5 = bf16[2,384,256]{1,2,0:T(8,128)(2,1)S(1)} fusion(bf16[2,384,384]{2,1,0:T(8,128)(2,1)} %param.31, bf16[2,384,384]{2,1,0:T(8,128)(2,1)} %param.29, bf16[2,384,256]{1,2,0:T(8,128)(2,1)} %copy.48, bf16[2,384,256]{1,2,0:T(8,128)(2,1)S(1)} %copy.50, pred[2,384]{1,0:T(4,128)(4,1)S(1)} %get-tuple-element.20, pred[2,384]{1,0:T(4,128)(4,1)S(1)} %iota_compare_fusion), kind=kOutput, calls=%fused_computation.14 | convolution fusion | flops 303169536 | bytes 2360832 | tf_op jit(solution)/shard_map/nji,nik->njk/dot_general | solution.py:26
  166.2 0.9 copy.52
  (39 shorter events, 0.2 us)
Async XLA Ops:
  0.6 128.6 %copy-start = (bf16[2,384,384]{2,1,0:T(8,128)(2,1)S(1)}, bf16[2,384,384]{2,1,0:T(8,128)(2,1)}, u32[]{:S(2)}) copy-start(bf16[2,384,384]{2,1,0:T(8,128)(2,1)} %param.26) | copy-start | bytes 1769476
  27.7 17.6 %copy-start.7 = (bf16[24,256]{1,0:T(8,128)(2,1)}, bf16[24,256]{1,0:T(8,128)(2,1)S(1)}, u32[]{:S(2)}) copy-start(bf16[24,256]{1,0:T(8,128)(2,1)S(1)} %convolution_convert_fusion.2) | copy-start | bytes 36868
  42.7 82.0 %copy-start.2 = (bf16[384,256]{1,0:T(8,128)(2,1)}, bf16[384,256]{1,0:T(8,128)(2,1)S(1)}, u32[]{:S(2)}) copy-start(bf16[384,256]{1,0:T(8,128)(2,1)S(1)} %all-gather) | copy-start | bytes 589828
  44.9 0.7 copy-start.10
  44.9 0.8 copy-start.9
  45.1 0.8 copy-start.8
  46.0 58.1 %copy-start.6 = (bf16[4,24,384]{2,1,0:T(8,128)(2,1)S(1)}, bf16[4,24,384]{2,1,0:T(8,128)(2,1)}, u32[]{:S(2)}) copy-start(bf16[4,24,384]{2,1,0:T(8,128)(2,1)} %param.21) | copy-start | bytes 221188
  104.1 21.6 %copy-start.12 = (s32[2]{0:T(128)S(1)}, s32[2]{0:T(128)}, u32[]{:S(2)}) copy-start(s32[2]{0:T(128)} %param.28) | copy-start | bytes 28
  104.1 21.9 %copy-start.11 = (s32[2,384]{1,0:T(2,128)S(1)}, s32[2,384]{1,0:T(2,128)}, u32[]{:S(2)}) copy-start(s32[2,384]{1,0:T(2,128)} %param.30) | copy-start | bytes 9220
  104.5 20.2 %copy-start.5 = (bf16[4,24,256]{2,1,0:T(8,128)(2,1)}, bf16[4,24,256]{2,1,0:T(8,128)(2,1)S(1)}, u32[]{:S(2)}) copy-start(bf16[4,24,256]{2,1,0:T(8,128)(2,1)S(1)} %fusion.7) | copy-start | bytes 147460
  124.7 0.9 copy-start.1
  126.1 2.9 %copy-start.3 = (bf16[2,384,256]{2,1,0:T(8,128)(2,1)S(1)}, bf16[2,384,256]{2,1,0:T(8,128)(2,1)}, u32[]{:S(2)}) copy-start(bf16[2,384,256]{2,1,0:T(8,128)(2,1)} %param.27) | copy-start | bytes 1179652
  126.1 3.2 %copy-start.14 = (bf16[2,384,384]{2,1,0:T(8,128)(2,1)S(1)}, bf16[2,384,384]{2,1,0:T(8,128)(2,1)}, u32[]{:S(2)}) copy-start(bf16[2,384,384]{2,1,0:T(8,128)(2,1)} %param.24) | copy-start | bytes 1769476
  128.8 17.4 %copy-start.13 = (s32[2]{0:T(128)S(1)}, s32[2]{0:T(128)}, u32[]{:S(2)}) copy-start(s32[2]{0:T(128)} %param.33) | copy-start | bytes 28
  129.0 18.2 %copy-start.4 = (bf16[2,384,256]{2,1,0:T(8,128)(2,1)S(1)}, bf16[2,384,256]{2,1,0:T(8,128)(2,1)}, u32[]{:S(2)}) copy-start(bf16[2,384,256]{2,1,0:T(8,128)(2,1)} %param.32) | copy-start | bytes 1179652
  129.9 18.2 %collective-permute-start = (bf16[2,384,256]{1,2,0:T(8,128)(2,1)S(1)}, bf16[2,384,256]{1,2,0:T(8,128)(2,1)}, u32[]{:S(2)}, u32[]{:S(2)}) collective-permute-start(bf16[2,384,256]{1,2,0:T(8,128)(2,1)S(1)} %fusion.6), channel_id=1, source_target_pairs={{510,0},{511,1},{0,2},{1,3},{2,4},{3,5},{4,6},{5,7},{6,8},{7,9},{8... | collective-permute-start | bytes 1179656 | tf_op jit(solution)/shard_map/ppermute | solution.py:12
  133.2 16.0 %collective-permute-start.1 = (bf16[2,384,256]{1,2,0:T(8,128)(2,1)S(1)}, bf16[2,384,256]{1,2,0:T(8,128)(2,1)}, u32[]{:S(2)}, u32[]{:S(2)}) collective-permute-start(bf16[2,384,256]{1,2,0:T(8,128)(2,1)S(1)} %fusion.6), channel_id=1, source_target_pairs={{511,0},{0,1},{1,2},{2,3},{3,4},{4,5},{5,6},{6,7},{7,8},{8,9},{9,1... | collective-permute-start | bytes 1179656 | tf_op jit(solution)/shard_map/ppermute | solution.py:12
  135.2 15.1 %collective-permute-start.2 = (bf16[2,384,256]{1,2,0:T(8,128)(2,1)S(1)}, bf16[2,384,256]{1,2,0:T(8,128)(2,1)}, u32[]{:S(2)}, u32[]{:S(2)}) collective-permute-start(bf16[2,384,256]{1,2,0:T(8,128)(2,1)S(1)} %fusion.6), channel_id=1, source_target_pairs={{1,0},{2,1},{3,2},{4,3},{5,4},{6,5},{7,6},{8,7},{9,8},{10,9},{11,1... | collective-permute-start | bytes 1179656 | tf_op jit(solution)/shard_map/ppermute | solution.py:12
  137.6 17.6 %collective-permute-start.3 = (bf16[2,384,256]{1,2,0:T(8,128)(2,1)S(1)}, bf16[2,384,256]{1,2,0:T(8,128)(2,1)S(1)}, u32[]{:S(2)}, u32[]{:S(2)}) collective-permute-start(bf16[2,384,256]{1,2,0:T(8,128)(2,1)S(1)} %fusion.6), channel_id=1, source_target_pairs={{2,0},{3,1},{4,2},{5,3},{6,4},{7,5},{8,6},{9,7},{10,8},{11,9},{12,... | collective-permute-start | bytes 1179656 | tf_op jit(solution)/shard_map/ppermute | solution.py:12
where the time goes:
time: 169 us; the launch traced here: 167 us
  blocking collectives  115 us (68%)
  local copies, waits for them, and re-layouts  22.1 us (13%)
  starting transfers between devices  16.3 us (10%)
  matrix products  5.26 us (3%)
  waiting for transfers between devices  3.77 us (2%)
  other arithmetic  3.61 us (2%)
    psum x1, blocking collectives, per_device(): mid_update = lax.psum(partials, 'front').astype(jnp.bfloat16)  54.5 us
    all_gather x2, blocking collectives, spread_solved(): return lax.all_gather(own_rows, 'front', axis=1, tiled=True)  35.2 us
    all_gather x1, blocking collectives, per_device(): rhs_whole = lax.all_gather(root_rhs, 'front', axis=0, tiled=True)  25.3 us
    ppermute x4, starting transfers between devices, from_behind(): return lax.ppermute(block, axis, route)  16.3 us
    gather x5, local copies, waits for them, and re-layouts, pick_rows(): picked = jnp.take(known_rows, row_index.reshape(-1), axis=0)  8.12 us
    unnamed x41, local copies, waits for them, and re-layouts  7.67 us
    ppermute x4, waiting for transfers between devices, from_behind(): return lax.ppermute(block, axis, route)  3.77 us
  transfers between devices with their start and end apart: 4, of which 1 were waited for; matrix products, arithmetic and copies ran while one was open for 3% of the time, Pallas kernels for 0%

commit v1 on v0

v1 whole, which is shorter than its diff:
```python
import functools

import jax
import jax.numpy as jnp
from jax import lax
from jax.experimental import pallas as pl
from jax.experimental.pallas import tpu as pltpu
from jax.sharding import Mesh, PartitionSpec as P

HOP = 2
ALL = ("y", "x", "z", "c")
ROWS = ("z", "c")
W = 384
K = 256
HALF = W // 2
LANE = 128
BF16 = jnp.bfloat16
F32 = jnp.float32

VMEM = pl.BlockSpec(memory_space=pltpu.VMEM)
SMEM = pl.BlockSpec(memory_space=pltpu.SMEM)
ANY = pl.BlockSpec(memory_space=pl.ANY)


def shape(*dims, dtype=BF16):
    return jax.ShapeDtypeStruct(dims, dtype)


def call(body, outs, ins, macs, moved, scratch=()):
    return pl.pallas_call(
        body,
        out_shape=outs,
        in_specs=ins,
        out_specs=jax.tree.map(lambda _: VMEM, outs),
        scratch_shapes=scratch,
        cost_estimate=pl.CostEstimate(flops=2 * macs, bytes_accessed=moved, transcendentals=0),
        compiler_params=pltpu.CompilerParams(vmem_limit_bytes=40 * 2**20),
    )


def dot(a, b):
    return jnp.dot(a, b, preferred_element_type=F32)


def one_hot(index_row, first, blocks):
    spread = jnp.broadcast_to(index_row, (LANE, W)).T
    lane = lax.broadcasted_iota(jnp.int32, (W, LANE), 1) + first
    parts = [(spread == lane + LANE * j).astype(F32).astype(BF16) for j in range(blocks)]
    return jnp.concatenate(parts, axis=1)


def upper_kernel(got, mid_index, root, part):
    side = lax.rem(lax.axis_index("y"), 2)
    core = lax.axis_index("c")
    solved = dot(got[:, :W], got[:, W : W + K]).astype(BF16)
    root[...] = solved
    picked = dot(one_hot(mid_index[...], 0, W // LANE), solved).astype(BF16)
    products = dot(got[:, W + 2 * K + LANE :].T, picked)
    first = pl.multiple_of(side * HALF, 64)
    rhs = got[pl.ds(first, HALF), W + K : W + 2 * K].astype(F32)
    update = (rhs - products[:HALF]).astype(BF16)
    head = update[:LANE]
    tail = jnp.concatenate([jnp.zeros((LANE // 2, K), BF16), update[LANE:]], axis=0)
    rows = pl.ds(pl.multiple_of(core * HALF, 64), HALF)
    inverse_head = got[rows, W + 2 * K : W + 2 * K + LANE]
    inverse_tail = got[rows, W + 2 * K + 2 * LANE :]
    part[...] = (dot(inverse_head, head) + dot(inverse_tail, tail)).astype(BF16)


def sub_ready_kernel(rows, panels, rhs, root, base, spread):
    for n in range(2):
        index = rows[n : n + 1, :]
        turned = panels[n].T
        picked = dot(one_hot(index, 0, W // LANE), root[...]).astype(BF16)
        base[n] = rhs[n].astype(F32) - dot(turned, picked)
        spread[n] = dot(turned, one_hot(index, W, W // LANE)).astype(BF16)


def sub_kernel(parents, mid, base, spread, inverse, out):
    here = lax.axis_index(ALL)
    for n in range(2):
        parent = parents[2 * here + n]
        above = mid[pl.ds(pl.multiple_of(parent * W, W), W), :]
        update = (base[n] - dot(spread[n], above)).astype(BF16)
        out[n] = dot(inverse[n], update).astype(BF16)


def leaf_ready_kernel(parents, groups, rows, panels, rhs, root, mid, base, spread):
    for n in range(2):
        index = rows[n : n + 1, :]
        parent = parents[groups[n]]
        above = mid[pl.ds(pl.multiple_of(parent * W, W), W), :]
        turned = panels[n].T
        picked = dot(one_hot(index, 0, W // LANE), root[...])
        picked += dot(one_hot(index, W, W // LANE), above)
        base[n] = rhs[n].astype(F32) - dot(turned, picked.astype(BF16))
        spread[n] = dot(turned, one_hot(index, 2 * W, W // LANE)).astype(BF16)


def leaf_kernel(total, groups, live, base, spread, inverse, *rest):
    sources = rest[: 2 * HOP + 1]
    out, held, sems = rest[2 * HOP + 1 :]
    here = lax.axis_index(ALL)
    for n in range(2):
        group = groups[n]
        slot = lax.rem(group // 2 - here + total + HOP, total)
        member = lax.rem(group, 2)
        for j, source in enumerate(sources):

            @pl.when(slot == j)
            def _():
                pltpu.make_async_copy(source.at[member], held.at[n], sems.at[n]).start()

    for n in range(2):
        pltpu.make_async_copy(sources[0].at[0], held.at[n], sems.at[n]).wait()
        update = (base[n] - dot(spread[n], held[n])).astype(BF16)
        solved = dot(inverse[n], update)
        row = lax.broadcasted_iota(jnp.int32, (W, K), 0)
        out[n] = jnp.where(row < live[n], solved, 0.0).astype(BF16)


def per_device(
    root_inverse,
    root_rhs,
    mid_panels,
    mid_rows,
    mid_inverse,
    mid_rhs,
    parent_list,
    sub_panels,
    sub_rows,
    sub_inverse,
    sub_rhs,
    group_of,
    leaf_panels,
    leaf_rows,
    leaf_inverse,
    leaf_rhs,
    live_cols,
):
    node = lax.axis_index("x")
    side = lax.rem(lax.axis_index("y"), 2)
    own_rows = root_inverse.shape[0]
    total = lax.axis_size(ALL)
    parents = parent_list.reshape(-1)

    def pick_node(array):
        return lax.dynamic_index_in_dim(array, node, 0, keepdims=False)

    def pick_side(array):
        return jnp.where(side == 0, array[:, :HALF], array[:, HALF:])

    panel, inverse = pick_side(pick_node(mid_panels)), pick_side(pick_node(mid_inverse))
    packed = jnp.concatenate(
        [
            root_inverse,
            root_rhs,
            pick_node(mid_rhs),
            inverse[:, :LANE],
            panel,
            inverse[:, LANE:],
        ],
        axis=1,
    )
    got = lax.all_gather(packed, ROWS, axis=0, tiled=True)
    mid_index = lax.dynamic_slice_in_dim(mid_rows, node, 1, 0)
    root, part = call(
        upper_kernel,
        (shape(W, K), shape(HALF, K)),
        [VMEM, VMEM],
        2 * W * W * K,
        2 * W * 1280,
    )(got, mid_index)
    other = lax.ppermute(part, "y", [(i, i ^ 1) for i in range(lax.axis_size("y"))])
    base, spread = call(
        sub_ready_kernel,
        (shape(2, W, K, dtype=F32), shape(2, W, W)),
        [VMEM] * 4,
        8 * W * W * K,
        8 * W * W + 24 * W * K,
    )(sub_rows, sub_panels, sub_rhs, root)
    mid_half = (part.astype(F32) + other.astype(F32)).astype(BF16)
    mid_half, base, spread = lax.optimization_barrier((mid_half, base, spread))
    mid = lax.all_gather(mid_half, ("x", "c"), axis=0, tiled=True)
    sub_solution = call(
        sub_kernel,
        shape(2, W, K),
        [SMEM] + [VMEM] * 4,
        4 * W * W * K,
        12 * W * W + 16 * W * K,
    )(parents, mid, base, spread, sub_inverse)
    nearby = {0: sub_solution}
    for offset in (2, -2, 1, -1):
        route = [((i + offset) % total, i) for i in range(total)]
        nearby[offset] = lax.ppermute(sub_solution, ALL, route)
    leaf_base, leaf_spread = call(
        leaf_ready_kernel,
        (shape(2, W, K, dtype=F32), shape(2, W, W)),
        [SMEM, SMEM] + [VMEM] * 5,
        12 * W * W * K,
        8 * W * W + 24 * W * K,
    )(parents, group_of, leaf_rows, leaf_panels, leaf_rhs, root, mid)
    leaf_solution = call(
        functools.partial(leaf_kernel, total),
        shape(2, W, K),
        [SMEM, SMEM] + [VMEM] * 3 + [ANY] * (2 * HOP + 1),
        4 * W * W * K,
        12 * W * W + 24 * W * K,
        scratch=[pltpu.VMEM((2, W, K), BF16), pltpu.SemaphoreType.DMA((2,))],
    )(
        group_of,
        live_cols,
        leaf_base,
        leaf_spread,
        leaf_inverse,
        *(nearby[offset] for offset in range(-HOP, HOP + 1)),
    )
    first = lax.axis_index(ROWS) * own_rows
    root_own = lax.dynamic_slice_in_dim(root, first, own_rows, 0)
    mid_own = lax.dynamic_slice_in_dim(mid.reshape(-1, W, K), first, own_rows, 1)
    return (root_own, mid_own, sub_solution, leaf_solution)


def solution(mesh):
    chips = Mesh(mesh.devices.reshape(8, 4, 8, 2), ALL)
    lower = P(ALL, None, None)
    return jax.shard_map(
        per_device,
        mesh=chips,
        in_specs=(
            P(ROWS, None),
            P(ROWS, None),
            P(None, ROWS, None),
            P(),
            P(None, ROWS, None),
            P(None, ROWS, None),
            P(),
            lower,
            P(ALL, None),
            lower,
            lower,
            P(ALL),
            lower,
            P(ALL, None),
            lower,
            lower,
            P(ALL),
        ),
        out_specs=(P(ROWS, None), P(None, ROWS, None), lower, lower),
        check_vma=False,
    )
```

time: 169 us -> 84.9 us (0.50)
  the two profiles are of different devices: /device:TPU:1 before, /device:TPU:32 now
where the time goes in v1:
time: 84.9 us; the launch traced here: 84.4 us
  blocking collectives  39.6 us (47%)
  starting transfers between devices  19.4 us (23%)
  Pallas kernels  10.6 us (12%)
  waiting for transfers between devices  7.86 us (9%)
  local copies, waits for them, and re-layouts  5.87 us (7%)
    all_gather x1, blocking collectives, per_device(): got = lax.all_gather(packed, ROWS, axis=0, tiled=True)  25.9 us
    ppermute x4, starting transfers between devices, per_device(): nearby[offset] = lax.ppermute(sub_solution, ALL, route)  16.8 us
    all_gather x1, blocking collectives, per_device(): mid = lax.all_gather(mid_half, ('x', 'c'), axis=0, tiled=True)  13.7 us
    ppermute x4, waiting for transfers between devices, per_device(): nearby[offset] = lax.ppermute(sub_solution, ALL, route)  5.05 us
    pallas_call x1, Pallas kernels, per_device(): call(functools.partial(leaf_kernel, total), shape(2, W, K), [SMEM, SMEM]...  3.17 us
    unnamed x32, local copies, waits for them, and re-layouts  3.01 us
    ppermute x1, waiting for transfers between devices, per_device(): lax.ppermute(part, 'y', [(i, i ^ 1) for i in range(lax.axis_size('y'))])  2.82 us
    pallas_call x1, Pallas kernels, per_device(): call(leaf_ready_kernel, (shape(2, W, K, dtype=F32), shape(2, W, W)), [SME...  2.68 us
  transfers between devices with their start and end apart: 5, of which 3 were waited for; matrix products, arithmetic and copies ran while one was open for 1% of the time, Pallas kernels for 5%

profile of v1, /device:TPU:32, one launch (start us, length us, event | category | flops | bytes accessed | tf_op | source)
XLA Modules:
  0.0 84.4 jit_solution(16736705526611904940)
XLA Ops:
  0.6 0.0 copy-start
  0.7 0.8 dynamic-slice_bitcast_fusion
  1.4 0.1 slice_select_fusion.1
  1.5 0.6 copy-done.13
  2.1 0.0 copy-done
  2.1 0.0 slice-start.1
  2.1 0.0 copy-start.14
  2.1 0.1 slice_select_fusion
  2.2 0.6 copy-done.15
  2.8 0.0 slice-done
  2.8 0.0 slice-done.1
  2.8 0.0 copy-done.14
  2.9 0.1 concatenate.3
  2.9 25.9 %all_gather.6.got = bf16[384,1280]{1,0:T(8,128)(2,1)S(1)} all-gather(bf16[24,1280]{1,0:T(8,128)(2,1)S(1)} %concatenate.3), channel_id=1, replica_groups=mesh['y'=8,'x'=4,'z'=8,'c'=2] {'z','c'}, dimensions={0}, use_global_device_ids=true | all-gather | bytes 1044480 | tf_op jit(solution)/shard_map/all_gather | solution.py:165
  28.8 0.8 constant_dynamic-slice_fusion.2.mid_index
  29.6 1.1 %shard_map.192 = (bf16[384,256]{1,0:T(8,128)(2,1)S(1)}, bf16[192,256]{1,0:T(8,128)(2,1)S(1)}) custom-call(bf16[384,1280]{1,0:T(8,128)(2,1)S(1)} %all_gather.6.got, s32[1,384]{1,0:T(1,128)S(1)} %constant_dynamic-slice_fusion.2.mid_index), custom_call_target="tpu_custom_call" | custom-call | flops 150994944 | bytes 983040 | tf_op jit(solution)/shard_map/pallas_call | solution.py:167
  30.7 0.0 copy-start.11
  30.7 2.6 %collective-permute-start = (bf16[192,256]{1,0:T(8,128)(2,1)S(1)}, bf16[192,256]{1,0:T(8,128)(2,1)S(1)}, u32[]{:S(2)}, u32[]{:S(2)}) collective-permute-start(bf16[192,256]{1,0:T(8,128)(2,1)S(1)} %get-tuple-element.14), channel_id=1, source_target_pairs={{0,64},{64,0},{128,192},{192,128},{256,320},{320,256},{384,448},{4... | collective-permute-start | bytes 294920 | tf_op jit(solution)/shard_map/ppermute | solution.py:174
  33.3 0.0 copy-done.7
  33.3 0.0 copy-done.9
  33.3 0.0 copy-done.11
  33.3 1.5 %shard_map.193 = (f32[2,384,256]{2,1,0:T(8,128)S(1)}, bf16[2,384,384]{2,1,0:T(8,128)(2,1)S(1)}) custom-call(s32[2,384]{1,0:T(2,128)S(1)} %copy-done.11, bf16[2,384,384]{2,1,0:T(8,128)(2,1)S(1)} %copy-done.7, bf16[2,384,256]{2,1,0:T(8,128)(2,1)S(1)} %copy-done.9, bf16[384,256]{1,0:T(8,128)(2,1)S(1)} %get-tuple-element.13.root), custom_call_target="tpu_custom_call" | custom-call | flops 603979776 | bytes 3538944 | tf_op jit(solution)/shard_map/pallas_call | solution.py:175
  34.8 0.0 copy-start.3
  34.8 2.8 %collective-permute-done = bf16[192,256]{1,0:T(8,128)(2,1)S(1)} collective-permute-done((bf16[192,256]{1,0:T(8,128)(2,1)S(1)}, bf16[192,256]{1,0:T(8,128)(2,1)S(1)}, u32[]{:S(2)}, u32[]{:S(2)}) %collective-permute-start) | collective-permute-done | bytes 98336 | tf_op jit(solution)/shard_map/ppermute | solution.py:174
  37.7 0.0 copy-start.4
  37.7 13.7 %all_gather.7.mid = bf16[1536,256]{1,0:T(8,128)(2,1)S(1)} all-gather(bf16[192,256]{1,0:T(8,128)(2,1)S(1)} %add_convert_fusion), channel_id=1, replica_groups=mesh['y'=8,'x'=4,'z'=8,'c'=2] {'x','c'}, dimensions={0}, use_global_device_ids=true | all-gather | bytes 884736 | tf_op jit(solution)/shard_map/all_gather | solution.py:184
  51.4 0.0 copy-done.3
  51.4 0.0 copy-done.4
  51.4 2.2 %shard_map.194.rest_2_ = bf16[2,384,256]{2,1,0:T(8,128)(2,1)} custom-call(s32[1024]{0:T(1024)S(1)} %bitcast.9, bf16[1536,256]{1,0:T(8,128)(2,1)S(1)} %all_gather.7.mid, f32[2,384,256]{2,1,0:T(8,128)S(1)} %get-tuple-element.18.base, bf16[2,384,384]{2,1,0:T(8,128)(2,1)S(1)} %get-tuple-element.19.spread, bf16[2,384,384]{2,1,0:T(8,128)(2,1)S(1)} %copy-done.3), custom_call_target="tpu_custom_call" | custom-call | flops 301989888 | bytes 3342336 | tf_op jit(solution)/shard_map/pallas_call | solution.py:185
  53.6 1.9 %collective-permute-start.1 = (bf16[2,384,256]{2,1,0:T(8,128)(2,1)}, bf16[2,384,256]{2,1,0:T(8,128)(2,1)S(1)}, u32[]{:S(2)}, u32[]{:S(2)}) collective-permute-start(bf16[2,384,256]{2,1,0:T(8,128)(2,1)} %shard_map.194.rest_2_), channel_id=1, source_target_pairs={{510,0},{511,1},{0,2},{1,3},{2,4},{3,5},{4,6},{5,7},{6,8},{7,9},{8... | collective-permute-start | bytes 1179656 | tf_op jit(solution)/shard_map/ppermute | solution.py:195
  55.5 2.3 %collective-permute-start.2 = (bf16[2,384,256]{2,1,0:T(8,128)(2,1)}, bf16[2,384,256]{2,1,0:T(8,128)(2,1)S(1)}, u32[]{:S(2)}, u32[]{:S(2)}) collective-permute-start(bf16[2,384,256]{2,1,0:T(8,128)(2,1)} %shard_map.194.rest_2_), channel_id=1, source_target_pairs={{511,0},{0,1},{1,2},{2,3},{3,4},{4,5},{5,6},{6,7},{7,8},{8,9},{9,1... | collective-permute-start | bytes 1179656 | tf_op jit(solution)/shard_map/ppermute | solution.py:195
  57.8 8.7 %collective-permute-start.3 = (bf16[2,384,256]{2,1,0:T(8,128)(2,1)}, bf16[2,384,256]{2,1,0:T(8,128)(2,1)S(1)}, u32[]{:S(2)}, u32[]{:S(2)}) collective-permute-start(bf16[2,384,256]{2,1,0:T(8,128)(2,1)} %shard_map.194.rest_2_), channel_id=1, source_target_pairs={{1,0},{2,1},{3,2},{4,3},{5,4},{6,5},{7,6},{8,7},{9,8},{10,9},{11,1... | collective-permute-start | bytes 1179656 | tf_op jit(solution)/shard_map/ppermute | solution.py:195
  66.6 3.9 %collective-permute-start.4 = (bf16[2,384,256]{2,1,0:T(8,128)(2,1)}, bf16[2,384,256]{2,1,0:T(8,128)(2,1)S(1)}, u32[]{:S(2)}, u32[]{:S(2)}) collective-permute-start(bf16[2,384,256]{2,1,0:T(8,128)(2,1)} %shard_map.194.rest_2_), channel_id=1, source_target_pairs={{2,0},{3,1},{4,2},{5,3},{6,4},{7,5},{8,6},{9,7},{10,8},{11,9},{12,... | collective-permute-start | bytes 1179656 | tf_op jit(solution)/shard_map/ppermute | solution.py:195
  70.5 0.0 copy-start.5
  70.5 0.0 copy-start.12
  70.5 0.6 constant_dynamic-slice_fusion.1
  71.1 0.0 copy-done.8
  71.1 0.0 copy-done.5
  71.1 0.0 copy-done.12
  71.2 1.0 %copy-done.10 = bf16[2,384,256]{2,1,0:T(8,128)(2,1)S(1)} copy-done((bf16[2,384,256]{2,1,0:T(8,128)(2,1)S(1)}, bf16[2,384,256]{2,1,0:T(8,128)(2,1)}, u32[]{:S(2)}) %copy-start.10) | copy-done | bytes 393240
  72.2 2.7 %shard_map.195 = (f32[2,384,256]{2,1,0:T(8,128)S(1)}, bf16[2,384,384]{2,1,0:T(8,128)(2,1)S(1)}) custom-call(s32[1024]{0:T(1024)S(1)} %bitcast.10, s32[2]{0:T(128)S(1)} %copy-done.5, s32[2,384]{1,0:T(2,128)S(1)} %copy-done.12, bf16[2,384,384]{2,1,0:T(8,128)(2,1)S(1)} %copy-done.8, bf16[2,384,256]{2,1,0:T(8,128)(2,1)S(1)} %copy-done.10, ...), custom_call_target="tpu_custom_call" | custom-call | flops 905969664 | bytes 3538944 | tf_op jit(solution)/shard_map/pallas_call | solution.py:196
  74.9 0.6 constant_dynamic-slice_fusion
  75.5 0.0 collective-permute-done.1.rest_0_
  75.5 1.2 %collective-permute-done.2.rest_1_ = bf16[2,384,256]{2,1,0:T(8,128)(2,1)S(1)} collective-permute-done((bf16[2,384,256]{2,1,0:T(8,128)(2,1)}, bf16[2,384,256]{2,1,0:T(8,128)(2,1)S(1)}, u32[]{:S(2)}, u32[]{:S(2)}) %collective-permute-start.2) | collective-permute-done | bytes 393248 | tf_op jit(solution)/shard_map/ppermute | solution.py:195
  76.7 0.0 collective-permute-done.3.rest_3_
  76.7 3.8 %collective-permute-done.4.rest_4_ = bf16[2,384,256]{2,1,0:T(8,128)(2,1)S(1)} collective-permute-done((bf16[2,384,256]{2,1,0:T(8,128)(2,1)}, bf16[2,384,256]{2,1,0:T(8,128)(2,1)S(1)}, u32[]{:S(2)}, u32[]{:S(2)}) %collective-permute-start.4) | collective-permute-done | bytes 393248 | tf_op jit(solution)/shard_map/ppermute | solution.py:195
  80.6 0.6 copy-done.6
  81.2 3.2 %shard_map.196 = bf16[2,384,256]{2,1,0:T(8,128)(2,1)} custom-call(s32[2]{0:T(128)S(1)} %copy-done.5, s32[2]{0:T(128)S(1)} %copy-done.6, f32[2,384,256]{2,1,0:T(8,128)S(1)} %get-tuple-element.20.base, bf16[2,384,384]{2,1,0:T(8,128)(2,1)S(1)} %get-tuple-element.21.spread, bf16[2,384,384]{2,1,0:T(8,128)(2,1)S(1)} %copy-done.2, ...), custom_call_target="tpu_custom_call" | custom-call | flops 301989888 | bytes 4128768 | tf_op jit(solution)/shard_map/pallas_call | solution.py:203
  (14 shorter events, 0.0 us)
Async XLA Ops:
  0.6 1.5 %copy-start = (bf16[4,24,256]{2,1,0:T(8,128)(2,1)S(1)}, bf16[4,24,256]{2,1,0:T(8,128)(2,1)}, u32[]{:S(2)}) copy-start(bf16[4,24,256]{2,1,0:T(8,128)(2,1)} %param.22) | copy-start | bytes 147460
  1.5 0.6 copy-start.13
  2.1 0.7 copy-start.15
  2.1 0.7 slice-start
  2.1 0.7 slice-start.1
  2.1 0.7 copy-start.14
  28.8 4.4 %copy-start.7 = (bf16[2,384,384]{2,1,0:T(8,128)(2,1)S(1)}, bf16[2,384,384]{2,1,0:T(8,128)(2,1)}, u32[]{:S(2)}) copy-start(bf16[2,384,384]{2,1,0:T(8,128)(2,1)} %panels.2) | copy-start | bytes 1769476
  29.6 3.7 %copy-start.9 = (bf16[2,384,256]{2,1,0:T(8,128)(2,1)S(1)}, bf16[2,384,256]{2,1,0:T(8,128)(2,1)}, u32[]{:S(2)}) copy-start(bf16[2,384,256]{2,1,0:T(8,128)(2,1)} %rhs.2) | copy-start | bytes 1179652
  30.7 2.6 %copy-start.11 = (s32[2,384]{1,0:T(2,128)S(1)}, s32[2,384]{1,0:T(2,128)}, u32[]{:S(2)}) copy-start(s32[2,384]{1,0:T(2,128)} %rows.2) | copy-start | bytes 9220
  30.7 6.9 %collective-permute-start = (bf16[192,256]{1,0:T(8,128)(2,1)S(1)}, bf16[192,256]{1,0:T(8,128)(2,1)S(1)}, u32[]{:S(2)}, u32[]{:S(2)}) collective-permute-start(bf16[192,256]{1,0:T(8,128)(2,1)S(1)} %get-tuple-element.14), channel_id=1, source_target_pairs={{0,64},{64,0},{128,192},{192,128},{256,320},{320,256},{384,448},{4... | collective-permute-start | bytes 294920 | tf_op jit(solution)/shard_map/ppermute | solution.py:174
  34.8 16.6 %copy-start.3 = (bf16[2,384,384]{2,1,0:T(8,128)(2,1)S(1)}, bf16[2,384,384]{2,1,0:T(8,128)(2,1)}, u32[]{:S(2)}) copy-start(bf16[2,384,384]{2,1,0:T(8,128)(2,1)} %inverse.2) | copy-start | bytes 1769476
  37.7 13.8 %copy-start.4 = (s32[1024,1]{0,1:T(1,128)S(1)}, s32[1024,1]{0,1:T(1,128)}, u32[]{:S(2)}) copy-start(s32[1024,1]{0,1:T(1,128)} %param.23) | copy-start | bytes 12292
  51.4 19.7 %copy-start.8 = (bf16[2,384,384]{2,1,0:T(8,128)(2,1)S(1)}, bf16[2,384,384]{2,1,0:T(8,128)(2,1)}, u32[]{:S(2)}) copy-start(bf16[2,384,384]{2,1,0:T(8,128)(2,1)} %panels.3) | copy-start | bytes 1769476
  53.6 21.9 %collective-permute-start.1 = (bf16[2,384,256]{2,1,0:T(8,128)(2,1)}, bf16[2,384,256]{2,1,0:T(8,128)(2,1)S(1)}, u32[]{:S(2)}, u32[]{:S(2)}) collective-permute-start(bf16[2,384,256]{2,1,0:T(8,128)(2,1)} %shard_map.194.rest_2_), channel_id=1, source_target_pairs={{510,0},{511,1},{0,2},{1,3},{2,4},{3,5},{4,6},{5,7},{6,8},{7,9},{8... | collective-permute-start | bytes 1179656 | tf_op jit(solution)/shard_map/ppermute | solution.py:195
  55.5 21.2 %collective-permute-start.2 = (bf16[2,384,256]{2,1,0:T(8,128)(2,1)}, bf16[2,384,256]{2,1,0:T(8,128)(2,1)S(1)}, u32[]{:S(2)}, u32[]{:S(2)}) collective-permute-start(bf16[2,384,256]{2,1,0:T(8,128)(2,1)} %shard_map.194.rest_2_), channel_id=1, source_target_pairs={{511,0},{0,1},{1,2},{2,3},{3,4},{4,5},{5,6},{6,7},{7,8},{8,9},{9,1... | collective-permute-start | bytes 1179656 | tf_op jit(solution)/shard_map/ppermute | solution.py:195
  57.8 18.9 %collective-permute-start.3 = (bf16[2,384,256]{2,1,0:T(8,128)(2,1)}, bf16[2,384,256]{2,1,0:T(8,128)(2,1)S(1)}, u32[]{:S(2)}, u32[]{:S(2)}) collective-permute-start(bf16[2,384,256]{2,1,0:T(8,128)(2,1)} %shard_map.194.rest_2_), channel_id=1, source_target_pairs={{1,0},{2,1},{3,2},{4,3},{5,4},{6,5},{7,6},{8,7},{9,8},{10,9},{11,1... | collective-permute-start | bytes 1179656 | tf_op jit(solution)/shard_map/ppermute | solution.py:195
  66.6 14.0 %collective-permute-start.4 = (bf16[2,384,256]{2,1,0:T(8,128)(2,1)}, bf16[2,384,256]{2,1,0:T(8,128)(2,1)S(1)}, u32[]{:S(2)}, u32[]{:S(2)}) collective-permute-start(bf16[2,384,256]{2,1,0:T(8,128)(2,1)} %shard_map.194.rest_2_), channel_id=1, source_target_pairs={{2,0},{3,1},{4,2},{5,3},{6,4},{7,5},{8,6},{9,7},{10,8},{11,9},{12,... | collective-permute-start | bytes 1179656 | tf_op jit(solution)/shard_map/ppermute | solution.py:195
  70.5 0.7 copy-start.5
  70.5 0.7 copy-start.12
  71.2 1.0 %copy-start.10 = (bf16[2,384,256]{2,1,0:T(8,128)(2,1)S(1)}, bf16[2,384,256]{2,1,0:T(8,128)(2,1)}, u32[]{:S(2)}) copy-start(bf16[2,384,256]{2,1,0:T(8,128)(2,1)} %rhs.3) | copy-start | bytes 1179652
  72.2 8.4 %copy-start.1 = (bf16[2,384,256]{2,1,0:T(8,128)(2,1)S(1)}, bf16[2,384,256]{2,1,0:T(8,128)(2,1)}, u32[]{:S(2)}) copy-start(bf16[2,384,256]{2,1,0:T(8,128)(2,1)} %shard_map.194.rest_2_) | copy-start | bytes 1179652
  72.2 8.4 %copy-start.2 = (bf16[2,384,384]{2,1,0:T(8,128)(2,1)S(1)}, bf16[2,384,384]{2,1,0:T(8,128)(2,1)}, u32[]{:S(2)}) copy-start(bf16[2,384,384]{2,1,0:T(8,128)(2,1)} %inverse.3) | copy-start | bytes 1769476
  80.6 0.7 copy-start.6

commit v2 on v1

v2 whole, which is shorter than its diff:
```python
import functools

import jax
import jax.numpy as jnp
from jax import lax
from jax.experimental import pallas as pl
from jax.experimental.pallas import tpu as pltpu
from jax.sharding import Mesh, PartitionSpec as P

HOP = 2
ALL = ("y", "x", "z", "c")
ROWS = ("z", "c")
W = 384
K = 256
HALF = W // 2
LANE = 128
BF16 = jnp.bfloat16
F32 = jnp.float32

VMEM = pl.BlockSpec(memory_space=pltpu.VMEM)
SMEM = pl.BlockSpec(memory_space=pltpu.SMEM)
ANY = pl.BlockSpec(memory_space=pl.ANY)
HBM = pl.BlockSpec(memory_space=pltpu.HBM)


def shape(*dims, dtype=BF16):
    return jax.ShapeDtypeStruct(dims, dtype)


def call(body, outs, ins, macs, moved, places=None, scratch=(), grant=16):
    return pl.pallas_call(
        body,
        out_shape=outs,
        in_specs=ins,
        out_specs=places or jax.tree.map(lambda _: VMEM, outs),
        scratch_shapes=scratch,
        cost_estimate=pl.CostEstimate(flops=2 * macs, bytes_accessed=moved, transcendentals=0),
        compiler_params=pltpu.CompilerParams(vmem_limit_bytes=int(grant * 2**20)),
    )


def dot(a, b):
    return jnp.dot(a, b, preferred_element_type=F32)


def one_hot(index_row, first, blocks):
    spread = jnp.broadcast_to(index_row, (LANE, W)).T
    lane = lax.broadcasted_iota(jnp.int32, (W, LANE), 1) + first
    parts = [(spread == lane + LANE * j).astype(F32).astype(BF16) for j in range(blocks)]
    return jnp.concatenate(parts, axis=1)


def pack_kernel(
    total,
    root_inverse,
    root_rhs,
    panels,
    inverses,
    rhs,
    parents_all,
    groups_all,
    live_all,
    out,
    facts,
    panel,
    inverse,
    parents,
    groups,
    live,
    sems,
):
    node = lax.axis_index("x")
    side = lax.rem(lax.axis_index("y"), 2)
    here = lax.axis_index(ALL)
    pairs = [
        (groups_all, groups),
        (parents_all, parents),
        (live_all, live),
        (panels.at[node], panel),
        (inverses.at[node], inverse),
        (root_inverse, out.at[:, :W]),
        (root_rhs, out.at[:, W : W + K]),
        (rhs.at[node], out.at[:, W + K : W + 2 * K]),
    ]
    copies = [pltpu.make_async_copy(a, b, sems.at[i]) for i, (a, b) in enumerate(pairs)]
    for copy in copies:
        copy.start()
    for copy in copies:
        copy.wait()
    values = []
    for n in range(2):
        group = groups[n]
        block = lax.rem(group // 2 - here + total + HOP, total) - HOP + lax.rem(here, 2)
        values += [parents[2 * here + n], parents[group], block, lax.rem(group, 2), live[n]]
    place = lax.broadcasted_iota(jnp.int32, facts.shape, 1)
    row = jnp.zeros(facts.shape, jnp.int32)
    for i, value in enumerate(values):
        row = jnp.where(place == i, value, row)
    facts[...] = row

    def half(array):
        return jnp.where(side == 0, array[:, :HALF], array[:, HALF:])

    inverse_half = half(inverse[...])
    out[:, W + 2 * K :] = jnp.concatenate(
        [inverse_half[:, :LANE], half(panel[...]), inverse_half[:, LANE:]], axis=1
    )


def upper_kernel(got, mid_rows, panels, inverses, root, part):
    del panels, inverses
    side = lax.rem(lax.axis_index("y"), 2)
    core = lax.axis_index("c")
    mid_index = mid_rows[pl.ds(lax.axis_index("x"), 1), :]
    solved = dot(got[:, :W], got[:, W : W + K]).astype(BF16)
    root[...] = solved
    picked = dot(one_hot(mid_index, 0, W // LANE), solved).astype(BF16)
    products = dot(got[:, W + 2 * K + LANE :].T, picked)
    first = pl.multiple_of(side * HALF, 64)
    rhs = got[pl.ds(first, HALF), W + K : W + 2 * K].astype(F32)
    update = (rhs - products[:HALF]).astype(BF16)
    head = update[:LANE]
    tail = jnp.concatenate([jnp.zeros((LANE // 2, K), BF16), update[LANE:]], axis=0)
    rows = pl.ds(pl.multiple_of(core * HALF, 64), HALF)
    inverse_head = got[rows, W + 2 * K : W + 2 * K + LANE]
    inverse_tail = got[rows, W + 2 * K + 2 * LANE :]
    part[...] = (dot(inverse_head, head) + dot(inverse_tail, tail)).astype(BF16)


def sub_ready_kernel(rows, panels, rhs, root, facts, base, spread):
    del facts
    for n in range(2):
        index = rows[n : n + 1, :]
        turned = panels[n].T
        picked = dot(one_hot(index, 0, W // LANE), root[...]).astype(BF16)
        base[n] = rhs[n].astype(F32) - dot(turned, picked)
        spread[n] = dot(turned, one_hot(index, W, W // LANE)).astype(BF16)


def rows_of(mid, parent):
    return mid[pl.ds(pl.multiple_of(parent * W, W), W), :]


def sub_kernel(facts, mid, base, spread, inverse, out):
    for n in range(2):
        update = (base[n] - dot(spread[n], rows_of(mid, facts[0, 5 * n]))).astype(BF16)
        out[n] = dot(inverse[n], update).astype(BF16)


def leaf_ready_kernel(
    facts, rows, panels, rhs, root, mid, solved, base, spread, root_own, mid_own, out, sem
):
    store = pltpu.make_async_copy(solved, out, sem)
    store.start()
    own_rows = root_own.shape[0]
    first = lax.axis_index(ROWS) * own_rows
    row = lax.broadcasted_iota(jnp.int32, (own_rows, W), 0) + first
    column = lax.broadcasted_iota(jnp.int32, (own_rows, W), 1)
    own = (row == column).astype(F32).astype(BF16)
    root_own[...] = dot(own, root[...]).astype(BF16)
    for s in range(mid_own.shape[0]):
        mid_own[s] = dot(own, mid[s * W : (s + 1) * W, :]).astype(BF16)
    for n in range(2):
        index = rows[n : n + 1, :]
        turned = panels[n].T
        picked = dot(one_hot(index, 0, W // LANE), root[...])
        picked += dot(one_hot(index, W, W // LANE), rows_of(mid, facts[0, 5 * n + 1]))
        base[n] = rhs[n].astype(F32) - dot(turned, picked.astype(BF16))
        spread[n] = dot(turned, one_hot(index, 2 * W, W // LANE)).astype(BF16)
    store.wait()


def leaf_kernel(facts, base, spread, inverse, chip, nearby, outer, out, held, done, sems):
    stores = []
    for n in range(2):
        block, member, live = (facts[0, 5 * n + i] for i in (2, 3, 4))

        @pl.when(jnp.logical_or(block == 0, block == 1))
        def _():
            held[n] = chip[2 * block + member]

        @pl.when(jnp.logical_or(block == -1, block == 2))
        def _():
            held[n] = nearby[jnp.where(block == 2, 0, 2) + member]

        @pl.when(jnp.logical_or(block == -2, block == 3))
        def _():
            held[n] = outer[member]

        update = (base[n] - dot(spread[n], held[n])).astype(BF16)
        solved = dot(inverse[n], update)
        row = lax.broadcasted_iota(jnp.int32, (W, K), 0)
        done[n] = jnp.where(row < live, solved, 0.0).astype(BF16)
        stores.append(pltpu.make_async_copy(done.at[n], out.at[n], sems.at[n]))
        stores[n].start()
    for store in stores:
        store.wait()


def per_device(
    root_inverse,
    root_rhs,
    mid_panels,
    mid_rows,
    mid_inverse,
    mid_rhs,
    parent_list,
    sub_panels,
    sub_rows,
    sub_inverse,
    sub_rhs,
    group_of,
    leaf_panels,
    leaf_rows,
    leaf_inverse,
    leaf_rhs,
    live_cols,
):
    own_rows = root_inverse.shape[0]
    total = lax.axis_size(ALL)
    parents = parent_list.reshape(-1)
    packed, facts = call(
        functools.partial(pack_kernel, total),
        (shape(own_rows, 1280), shape(1, LANE, dtype=jnp.int32)),
        [HBM] * 8,
        0,
        4 * own_rows * 1280,
        scratch=[pltpu.VMEM((own_rows, W), BF16)] * 2
        + [pltpu.SMEM(a.shape, jnp.int32) for a in (parents, group_of, live_cols)]
        + [pltpu.SemaphoreType.DMA((8,))],
        grant=60,
    )(root_inverse, root_rhs, mid_panels, mid_inverse, mid_rhs, parents, group_of, live_cols)
    got = lax.all_gather(packed, ROWS, axis=0, tiled=True)
    square, tall = shape(2, W, W), shape(2, W, K, dtype=F32)
    thin = shape(2, W, K)
    root, part = call(
        upper_kernel,
        (shape(W, K), shape(HALF, K)),
        [VMEM] * 4,
        2 * W * W * K,
        2 * W * 1280,
    )(got, mid_rows, leaf_panels, leaf_inverse)
    other = lax.ppermute(part, "y", [(i, i ^ 1) for i in range(lax.axis_size("y"))])
    base, spread = call(
        sub_ready_kernel,
        (tall, square),
        [VMEM] * 5,
        8 * W * W * K,
        8 * W * W + 24 * W * K,
    )(sub_rows, sub_panels, sub_rhs, root, facts)
    mid_half = (part.astype(F32) + other.astype(F32)).astype(BF16)
    mid_half, base = lax.optimization_barrier((mid_half, base))
    mid = lax.all_gather(mid_half, ("x", "c"), axis=0, tiled=True)
    solved = call(
        sub_kernel,
        shape(2, W, K),
        [SMEM] + [VMEM] * 4,
        4 * W * W * K,
        12 * W * W + 16 * W * K,
    )(facts, mid, base, spread, sub_inverse)
    chips = total // 2
    up = [((2 * m + 2 + c) % total, 2 * m + c) for m in range(chips) for c in range(2)]
    down = [((2 * m - 2 + c) % total, 2 * m + c) for m in range(chips) for c in range(2)]
    inner = lax.ppermute(solved, ALL, up[0::2] + down[1::2])
    outer = lax.ppermute(solved, ALL, down[0::2] + up[1::2])
    chip = lax.all_gather(solved, "c", axis=0, tiled=True)
    leaf_base, leaf_spread, root_own, mid_own, sub_solution = call(
        leaf_ready_kernel,
        (tall, square, shape(own_rows, K), shape(mid_rows.shape[0], own_rows, K), thin),
        [SMEM] + [VMEM] * 6,
        12 * W * W * K,
        8 * W * W + 24 * W * K,
        places=(VMEM,) * 4 + (HBM,),
        scratch=[pltpu.SemaphoreType.DMA],
    )(facts, leaf_rows, leaf_panels, leaf_rhs, root, mid, solved)
    inner, chip, leaf_base = lax.optimization_barrier((inner, chip, leaf_base))
    nearby = lax.all_gather(inner, "c", axis=0, tiled=True)
    leaf_solution = call(
        leaf_kernel,
        shape(2, W, K),
        [SMEM] + [VMEM] * 6,
        4 * W * W * K,
        12 * W * W + 24 * W * K,
        places=HBM,
        scratch=[pltpu.VMEM((2, W, K), BF16)] * 2 + [pltpu.SemaphoreType.DMA((2,))],
    )(facts, leaf_base, leaf_spread, leaf_inverse, chip, nearby, outer)
    return (root_own, mid_own, sub_solution, leaf_solution)


def solution(mesh):
    chips = Mesh(mesh.devices.reshape(8, 4, 8, 2), ALL)
    lower = P(ALL, None, None)
    return jax.shard_map(
        per_device,
        mesh=chips,
        in_specs=(
            P(ROWS, None),
            P(ROWS, None),
            P(None, ROWS, None),
            P(),
            P(None, ROWS, None),
            P(None, ROWS, None),
            P(),
            lower,
            P(ALL, None),
            lower,
            lower,
            P(ALL),
            lower,
            P(ALL, None),
            lower,
            lower,
            P(ALL),
        ),
        out_specs=(P(ROWS, None), P(None, ROWS, None), lower, lower),
        check_vma=False,
    )
```

time: 84.9 us -> 74.8 us (0.88)
  the two profiles are of different devices: /device:TPU:32 before, /device:TPU:1 now
where the time goes in v2:
time: 74.8 us; the launch traced here: 74.5 us
  blocking collectives  46.8 us (63%)
  starting transfers between devices  13.9 us (19%)
  Pallas kernels  11.6 us (16%)
  between operations  0.81 us (1%)
  waiting for transfers between devices  0.77 us (1%)
    all_gather x1, blocking collectives, per_device(): got = lax.all_gather(packed, ROWS, axis=0, tiled=True)  27.5 us
    all_gather x1, blocking collectives, per_device(): mid = lax.all_gather(mid_half, ('x', 'c'), axis=0, tiled=True)  14.5 us
    ppermute x1, starting transfers between devices, per_device(): outer = lax.ppermute(solved, ALL, down[0::2] + up[1::2])  8.79 us
    pallas_call x1, Pallas kernels, per_device(): call(leaf_ready_kernel, (tall, square, shape(own_rows, K), shape(mid_rows...  3.35 us
    ppermute x1, starting transfers between devices, per_device(): lax.ppermute(part, 'y', [(i, i ^ 1) for i in range(lax.axis_size('y'))])  3.21 us
    pallas_call x1, Pallas kernels, per_device(): call(leaf_kernel, shape(2, W, K), [SMEM] + [VMEM] * 6, 4 * W * W * K, 12...  2.57 us
    all_gather x1, blocking collectives, per_device(): chip = lax.all_gather(solved, 'c', axis=0, tiled=True)  2.37 us
    all_gather x1, blocking collectives, per_device(): nearby = lax.all_gather(inner, 'c', axis=0, tiled=True)  2.36 us
  transfers between devices with their start and end apart: 3, of which 1 were waited for; matrix products, arithmetic and copies ran while one was open for 0% of the time, Pallas kernels for 6%

profile of v2, /device:TPU:1, one launch (start us, length us, event | category | flops | bytes accessed | tf_op | source)
XLA Modules:
  0.0 74.5 jit_solution(2752119623670495339)
XLA Ops:
  0.6 0.0 copy-start
  0.6 0.0 copy-start.1
  0.7 1.7 %shard_map.192 = (bf16[24,1280]{1,0:T(8,128)(2,1)}, s32[1,128]{1,0:T(1,128)}) custom-call(bf16[24,384]{1,0:T(8,128)(2,1)} %root_inverse.1, bf16[24,256]{1,0:T(8,128)(2,1)} %root_rhs.1, bf16[4,24,384]{2,1,0:T(8,128)(2,1)} %panels.4, bf16[4,24,384]{2,1,0:T(8,128)(2,1)} %inverses.2, bf16[4,24,256]{2,1,0:T(8,128)(2,1)} %rhs.3, s32[1024]{0:T(1024)} %bitcast.1, ...), custom_call_target="tpu_custom_call" | custom-call | bytes 122880 | tf_op jit(solution)/shard_map/pallas_call | solution.py:222
  2.4 0.0 copy-start.3
  2.4 27.5 %all_gather.12.got = bf16[384,1280]{1,0:T(8,128)(2,1)S(1)} all-gather(bf16[24,1280]{1,0:T(8,128)(2,1)} %get-tuple-element.21), channel_id=1, replica_groups=mesh['y'=8,'x'=4,'z'=8,'c'=2] {'z','c'}, dimensions={0}, use_global_device_ids=true | all-gather | bytes 1044480 | tf_op jit(solution)/shard_map/all_gather | solution.py:233
  29.9 0.0 copy-done
  29.9 0.0 copy-done.1
  29.9 0.0 copy-done.3
  29.9 0.0 copy-start.5
  29.9 0.0 copy-start.6
  29.9 1.1 %shard_map.193 = (bf16[384,256]{1,0:T(8,128)(2,1)S(1)}, bf16[192,256]{1,0:T(8,128)(2,1)S(1)}) custom-call(bf16[384,1280]{1,0:T(8,128)(2,1)S(1)} %all_gather.12.got, s32[4,384]{1,0:T(4,128)S(1)} %copy-done.3, bf16[2,384,384]{2,1,0:T(8,128)(2,1)S(1)} %copy-done.1, bf16[2,384,384]{2,1,0:T(8,128)(2,1)S(1)} %copy-done), custom_call_target="tpu_custom_call" | custom-call | flops 150994944 | bytes 983040 | tf_op jit(solution)/shard_map/pallas_call | solution.py:236
  31.0 0.0 copy-start.8
  31.0 3.2 %collective-permute-start = (bf16[192,256]{1,0:T(8,128)(2,1)S(1)}, bf16[192,256]{1,0:T(8,128)(2,1)S(1)}, u32[]{:S(2)}, u32[]{:S(2)}) collective-permute-start(bf16[192,256]{1,0:T(8,128)(2,1)S(1)} %get-tuple-element.23), channel_id=1, source_target_pairs={{0,64},{64,0},{128,192},{192,128},{256,320},{320,256},{384,448},{4... | collective-permute-start | bytes 294920 | tf_op jit(solution)/shard_map/ppermute | solution.py:243
  34.2 0.0 copy-start.4
  34.2 0.0 copy-done.5
  34.3 0.0 copy-done.6
  34.3 0.0 copy-done.8
  34.3 0.6 copy-done.4
  34.9 1.5 %shard_map.194 = (f32[2,384,256]{2,1,0:T(8,128)S(1)}, bf16[2,384,384]{2,1,0:T(8,128)(2,1)S(1)}) custom-call(s32[2,384]{1,0:T(2,128)S(1)} %copy-done.8, bf16[2,384,384]{2,1,0:T(8,128)(2,1)S(1)} %copy-done.5, bf16[2,384,256]{2,1,0:T(8,128)(2,1)S(1)} %copy-done.6, bf16[384,256]{1,0:T(8,128)(2,1)S(1)} %get-tuple-element.22.root, s32[1,128]{1,0:T(1,128)S(1)} %copy-done.4), custom_call_target="tpu_custom_call" | custom-call | flops 603979776 | bytes 3538944 | tf_op jit(solution)/shard_map/pallas_call | solution.py:244
  36.4 0.0 copy-start.2
  36.4 0.8 %collective-permute-done = bf16[192,256]{1,0:T(8,128)(2,1)S(1)} collective-permute-done((bf16[192,256]{1,0:T(8,128)(2,1)S(1)}, bf16[192,256]{1,0:T(8,128)(2,1)S(1)}, u32[]{:S(2)}, u32[]{:S(2)}) %collective-permute-start) | collective-permute-done | bytes 98336 | tf_op jit(solution)/shard_map/ppermute | solution.py:243
  37.2 14.5 %all_gather.13.mid = bf16[1536,256]{1,0:T(8,128)(2,1)S(1)} all-gather(bf16[192,256]{1,0:T(8,128)(2,1)S(1)} %add_convert_fusion), channel_id=1, replica_groups=mesh['y'=8,'x'=4,'z'=8,'c'=2] {'x','c'}, dimensions={0}, use_global_device_ids=true | all-gather | bytes 884736 | tf_op jit(solution)/shard_map/all_gather | solution.py:253
  51.7 0.0 copy-done.2
  51.7 0.0 copy-start.7
  51.7 0.0 copy-start.9
  51.7 1.4 %shard_map.195.solved = bf16[2,384,256]{2,1,0:T(8,128)(2,1)S(1)} custom-call(s32[1,128]{1,0:T(1,128)S(1)} %copy-done.4, bf16[1536,256]{1,0:T(8,128)(2,1)S(1)} %all_gather.13.mid, f32[2,384,256]{2,1,0:T(8,128)S(1)} %get-tuple-element.26.base, bf16[2,384,384]{2,1,0:T(8,128)(2,1)S(1)} %get-tuple-element.27.spread, bf16[2,384,384]{2,1,0:T(8,128)(2,1)S(1)} %copy-done.2), custom_call_target="tpu_custom_call" | custom-call | flops 301989888 | bytes 3342336 | tf_op jit(solution)/shard_map/pallas_call | solution.py:254
  53.1 1.9 %collective-permute-start.1 = (bf16[2,384,256]{2,1,0:T(8,128)(2,1)S(1)}, bf16[2,384,256]{2,1,0:T(8,128)(2,1)S(1)}, u32[]{:S(2)}, u32[]{:S(2)}) collective-permute-start(bf16[2,384,256]{2,1,0:T(8,128)(2,1)S(1)} %shard_map.195.solved), channel_id=1, source_target_pairs={{2,0},{4,2},{6,4},{8,6},{10,8},{12,10},{14,12},{16,14},{18,16},{20... | collective-permute-start | bytes 1179656 | tf_op jit(solution)/shard_map/ppermute | solution.py:264
  55.1 8.8 %collective-permute-start.2 = (bf16[2,384,256]{2,1,0:T(8,128)(2,1)S(1)}, bf16[2,384,256]{2,1,0:T(8,128)(2,1)S(1)}, u32[]{:S(2)}, u32[]{:S(2)}) collective-permute-start(bf16[2,384,256]{2,1,0:T(8,128)(2,1)S(1)} %shard_map.195.solved), channel_id=1, source_target_pairs={{510,0},{0,2},{2,4},{4,6},{6,8},{8,10},{10,12},{12,14},{14,16},{16... | collective-permute-start | bytes 1179656 | tf_op jit(solution)/shard_map/ppermute | solution.py:265
  63.9 0.0 copy-done.7
  63.9 0.0 copy-done.9
  63.9 3.4 %shard_map.196 = (f32[2,384,256]{2,1,0:T(8,128)S(1)}, bf16[2,384,384]{2,1,0:T(8,128)(2,1)S(1)}, bf16[24,256]{1,0:T(8,128)(2,1)}, bf16[4,24,256]{2,1,0:T(8,128)(2,1)}, bf16[2,384,256]{2,1,0:T(8,128)(2,1)}) custom-call(s32[1,128]{1,0:T(1,128)S(1)} %copy-done.4, s32[2,384]{1,0:T(2,128)S(1)} %copy-done.9, bf16[2,384,384]{2,1,0:T(8,128)(2,1)S(1)} %copy-done.1, ...), custom_call_target="tpu_custom_call" | custom-call | flops 905969664 | bytes 3538944 | tf_op jit(solution)/shard_map/pallas_call | solution.py:267
  67.2 2.4 %all_gather.14.chip = bf16[4,384,256]{2,1,0:T(8,128)(2,1)S(1)} all-gather(bf16[2,384,256]{2,1,0:T(8,128)(2,1)S(1)} %shard_map.195.solved), channel_id=1, replica_groups=mesh['y'=8,'x'=4,'z'=8,'c'=2] {'c'}, dimensions={0}, use_global_device_ids=true | all-gather | bytes 1179648 | tf_op jit(solution)/shard_map/all_gather | solution.py:266
  69.6 0.0 collective-permute-done.1
  69.6 2.4 %all_gather.15.nearby = bf16[4,384,256]{2,1,0:T(8,128)(2,1)S(1)} all-gather(bf16[2,384,256]{2,1,0:T(8,128)(2,1)S(1)} %collective-permute-done.1), channel_id=1, replica_groups=mesh['y'=8,'x'=4,'z'=8,'c'=2] {'c'}, dimensions={0}, use_global_device_ids=true | all-gather | bytes 1179648 | tf_op jit(solution)/shard_map/all_gather | solution.py:277
  72.0 0.0 collective-permute-done.2.outer
  72.0 2.6 %shard_map.197 = bf16[2,384,256]{2,1,0:T(8,128)(2,1)} custom-call(s32[1,128]{1,0:T(1,128)S(1)} %copy-done.4, f32[2,384,256]{2,1,0:T(8,128)S(1)} %get-tuple-element.32.base, bf16[2,384,384]{2,1,0:T(8,128)(2,1)S(1)} %get-tuple-element.33.spread, bf16[2,384,384]{2,1,0:T(8,128)(2,1)S(1)} %copy-done, bf16[4,384,256]{2,1,0:T(8,128)(2,1)S(1)} %all_gather.14.chip, ...), custom_call_target="tpu_custom_call" | custom-call | flops 301989888 | bytes 4128768 | tf_op jit(solution)/shard_map/pallas_call | solution.py:278
  (1 shorter events, 0.0 us)
Async XLA Ops:
  0.6 29.3 %copy-start = (bf16[2,384,384]{2,1,0:T(8,128)(2,1)S(1)}, bf16[2,384,384]{2,1,0:T(8,128)(2,1)}, u32[]{:S(2)}) copy-start(bf16[2,384,384]{2,1,0:T(8,128)(2,1)} %inverse.3) | copy-start | bytes 1769476
  0.6 29.3 %copy-start.1 = (bf16[2,384,384]{2,1,0:T(8,128)(2,1)S(1)}, bf16[2,384,384]{2,1,0:T(8,128)(2,1)}, u32[]{:S(2)}) copy-start(bf16[2,384,384]{2,1,0:T(8,128)(2,1)} %panels.7) | copy-start | bytes 1769476
  2.4 27.5 %copy-start.3 = (s32[4,384]{1,0:T(4,128)S(1)}, s32[4,384]{1,0:T(4,128)}, u32[]{:S(2)}) copy-start(s32[4,384]{1,0:T(4,128)} %mid_rows.1) | copy-start | bytes 18436
  29.9 4.3 %copy-start.5 = (bf16[2,384,384]{2,1,0:T(8,128)(2,1)S(1)}, bf16[2,384,384]{2,1,0:T(8,128)(2,1)}, u32[]{:S(2)}) copy-start(bf16[2,384,384]{2,1,0:T(8,128)(2,1)} %panels.6) | copy-start | bytes 1769476
  29.9 4.3 %copy-start.6 = (bf16[2,384,256]{2,1,0:T(8,128)(2,1)S(1)}, bf16[2,384,256]{2,1,0:T(8,128)(2,1)}, u32[]{:S(2)}) copy-start(bf16[2,384,256]{2,1,0:T(8,128)(2,1)} %rhs.4) | copy-start | bytes 1179652
  31.0 3.3 %copy-start.8 = (s32[2,384]{1,0:T(2,128)S(1)}, s32[2,384]{1,0:T(2,128)}, u32[]{:S(2)}) copy-start(s32[2,384]{1,0:T(2,128)} %rows.2) | copy-start | bytes 9220
  31.0 6.1 %collective-permute-start = (bf16[192,256]{1,0:T(8,128)(2,1)S(1)}, bf16[192,256]{1,0:T(8,128)(2,1)S(1)}, u32[]{:S(2)}, u32[]{:S(2)}) collective-permute-start(bf16[192,256]{1,0:T(8,128)(2,1)S(1)} %get-tuple-element.23), channel_id=1, source_target_pairs={{0,64},{64,0},{128,192},{192,128},{256,320},{320,256},{384,448},{4... | collective-permute-start | bytes 294920 | tf_op jit(solution)/shard_map/ppermute | solution.py:243
  34.2 0.7 copy-start.4
  36.4 15.3 %copy-start.2 = (bf16[2,384,384]{2,1,0:T(8,128)(2,1)S(1)}, bf16[2,384,384]{2,1,0:T(8,128)(2,1)}, u32[]{:S(2)}) copy-start(bf16[2,384,384]{2,1,0:T(8,128)(2,1)} %inverse.2) | copy-start | bytes 1769476
  51.7 12.1 %copy-start.7 = (bf16[2,384,256]{2,1,0:T(8,128)(2,1)S(1)}, bf16[2,384,256]{2,1,0:T(8,128)(2,1)}, u32[]{:S(2)}) copy-start(bf16[2,384,256]{2,1,0:T(8,128)(2,1)} %rhs.5) | copy-start | bytes 1179652
  51.7 12.1 %copy-start.9 = (s32[2,384]{1,0:T(2,128)S(1)}, s32[2,384]{1,0:T(2,128)}, u32[]{:S(2)}) copy-start(s32[2,384]{1,0:T(2,128)} %rows.3) | copy-start | bytes 9220
  53.1 16.5 %collective-permute-start.1 = (bf16[2,384,256]{2,1,0:T(8,128)(2,1)S(1)}, bf16[2,384,256]{2,1,0:T(8,128)(2,1)S(1)}, u32[]{:S(2)}, u32[]{:S(2)}) collective-permute-start(bf16[2,384,256]{2,1,0:T(8,128)(2,1)S(1)} %shard_map.195.solved), channel_id=1, source_target_pairs={{2,0},{4,2},{6,4},{8,6},{10,8},{12,10},{14,12},{16,14},{18,16},{20... | collective-permute-start | bytes 1179656 | tf_op jit(solution)/shard_map/ppermute | solution.py:264
  55.1 16.9 %collective-permute-start.2 = (bf16[2,384,256]{2,1,0:T(8,128)(2,1)S(1)}, bf16[2,384,256]{2,1,0:T(8,128)(2,1)S(1)}, u32[]{:S(2)}, u32[]{:S(2)}) collective-permute-start(bf16[2,384,256]{2,1,0:T(8,128)(2,1)S(1)} %shard_map.195.solved), channel_id=1, source_target_pairs={{510,0},{0,2},{2,4},{4,6},{6,8},{8,10},{10,12},{12,14},{14,16},{16... | collective-permute-start | bytes 1179656 | tf_op jit(solution)/shard_map/ppermute | solution.py:265

commit v3 on v2

--- a/solution.py
+++ b/solution.py
@@ -127,7 +127,9 @@
     part[...] = (dot(inverse_head, head) + dot(inverse_tail, tail)).astype(BF16)
 
 
-def sub_ready_kernel(rows, panels, rhs, root, facts, base, spread):
+def ready_kernel(
+    rows, panels, rhs, root, facts, low_rows, low_panels, base, spread, low_base, low_spread
+):
     del facts
     for n in range(2):
         index = rows[n : n + 1, :]
@@ -135,6 +137,12 @@
         picked = dot(one_hot(index, 0, W // LANE), root[...]).astype(BF16)
         base[n] = rhs[n].astype(F32) - dot(turned, picked)
         spread[n] = dot(turned, one_hot(index, W, W // LANE)).astype(BF16)
+    for n in range(2):
+        index = low_rows[n : n + 1, :]
+        turned = low_panels[n].T
+        picked = dot(one_hot(index, 0, W // LANE), root[...]).astype(BF16)
+        low_base[n] = dot(turned, picked)
+        low_spread[n] = dot(turned, one_hot(index, 2 * W, W // LANE)).astype(BF16)
 
 
 def rows_of(mid, parent):
@@ -147,8 +155,8 @@
         out[n] = dot(inverse[n], update).astype(BF16)
 
 
-def leaf_ready_kernel(
-    facts, rows, panels, rhs, root, mid, solved, base, spread, root_own, mid_own, out, sem
+def leaf_middle_kernel(
+    facts, rows, panels, rhs, root, mid, solved, from_root, base, root_own, mid_own, out, sem
 ):
     store = pltpu.make_async_copy(solved, out, sem)
     store.start()
@@ -162,11 +170,9 @@
         mid_own[s] = dot(own, mid[s * W : (s + 1) * W, :]).astype(BF16)
     for n in range(2):
         index = rows[n : n + 1, :]
-        turned = panels[n].T
-        picked = dot(one_hot(index, 0, W // LANE), root[...])
-        picked += dot(one_hot(index, W, W // LANE), rows_of(mid, facts[0, 5 * n + 1]))
-        base[n] = rhs[n].astype(F32) - dot(turned, picked.astype(BF16))
-        spread[n] = dot(turned, one_hot(index, 2 * W, W // LANE)).astype(BF16)
+        above = rows_of(mid, facts[0, 5 * n + 1])
+        picked = dot(one_hot(index, W, W // LANE), above).astype(BF16)
+        base[n] = rhs[n].astype(F32) - from_root[n] - dot(panels[n].T, picked)
     store.wait()
 
 
@@ -181,7 +187,7 @@
 
         @pl.when(jnp.logical_or(block == -1, block == 2))
         def _():
-            held[n] = nearby[jnp.where(block == 2, 0, 2) + member]
+            held[n] = nearby[jnp.where(block == 2, 2, 0) + member]
 
         @pl.when(jnp.logical_or(block == -2, block == 3))
         def _():
@@ -241,13 +247,13 @@
         2 * W * 1280,
     )(got, mid_rows, leaf_panels, leaf_inverse)
     other = lax.ppermute(part, "y", [(i, i ^ 1) for i in range(lax.axis_size("y"))])
-    base, spread = call(
-        sub_ready_kernel,
-        (tall, square),
-        [VMEM] * 5,
-        8 * W * W * K,
-        8 * W * W + 24 * W * K,
-    )(sub_rows, sub_panels, sub_rhs, root, facts)
+    base, spread, from_root, leaf_spread = call(
+        ready_kernel,
+        (tall, square, tall, square),
+        [VMEM] * 7,
+        16 * W * W * K,
+        16 * W * W + 40 * W * K,
+    )(sub_rows, sub_panels, sub_rhs, root, facts, leaf_rows, leaf_panels)
     mid_half = (part.astype(F32) + other.astype(F32)).astype(BF16)
     mid_half, base = lax.optimization_barrier((mid_half, base))
     mid = lax.all_gather(mid_half, ("x", "c"), axis=0, tiled=True)
@@ -259,20 +265,22 @@
         12 * W * W + 16 * W * K,
     )(facts, mid, base, spread, sub_inverse)
     chips = total // 2
-    up = [((2 * m + 2 + c) % total, 2 * m + c) for m in range(chips) for c in range(2)]
-    down = [((2 * m - 2 + c) % total, 2 * m + c) for m in range(chips) for c in range(2)]
-    inner = lax.ppermute(solved, ALL, up[0::2] + down[1::2])
-    outer = lax.ppermute(solved, ALL, down[0::2] + up[1::2])
+    cross = [((2 * m - 1) % total, 2 * m) for m in range(chips)]
+    cross += [((2 * m + 2) % total, 2 * m + 1) for m in range(chips)]
+    straight = [((2 * m - 2) % total, 2 * m) for m in range(chips)]
+    straight += [((2 * m + 3) % total, 2 * m + 1) for m in range(chips)]
+    inner = lax.ppermute(solved, ALL, cross)
+    outer = lax.ppermute(solved, ALL, straight)
     chip = lax.all_gather(solved, "c", axis=0, tiled=True)
-    leaf_base, leaf_spread, root_own, mid_own, sub_solution = call(
-        leaf_ready_kernel,
-        (tall, square, shape(own_rows, K), shape(mid_rows.shape[0], own_rows, K), thin),
-        [SMEM] + [VMEM] * 6,
-        12 * W * W * K,
+    leaf_base, root_own, mid_own, sub_solution = call(
+        leaf_middle_kernel,
+        (tall, shape(own_rows, K), shape(mid_rows.shape[0], own_rows, K), thin),
+        [SMEM] + [VMEM] * 7,
+        4 * W * W * K,
         8 * W * W + 24 * W * K,
-        places=(VMEM,) * 4 + (HBM,),
+        places=(VMEM,) * 3 + (HBM,),
         scratch=[pltpu.SemaphoreType.DMA],
-    )(facts, leaf_rows, leaf_panels, leaf_rhs, root, mid, solved)
+    )(facts, leaf_rows, leaf_panels, leaf_rhs, root, mid, solved, from_root)
     inner, chip, leaf_base = lax.optimization_barrier((inner, chip, leaf_base))
     nearby = lax.all_gather(inner, "c", axis=0, tiled=True)
     leaf_solution = call(

time: 74.8 us -> 73.8 us (0.987)
  waiting for transfers between devices: 0.77 us -> 0.01 us
    ppermute x1, waiting for transfers between devices: 0.77 us -> 0.01 us  [per_device(): lax.ppermute(part, 'y', [(i, i ^ 1) for i in range(lax.axis_size('y'))])]
  transfers between devices with their start and end apart: 3 -> 3, of which waited for: 1 -> 0; matrix products, arithmetic and copies ran while one was open for 0% -> 0% of each run, Pallas kernels for 6% -> 7%
where the time goes in v3:
time: 73.8 us; the launch traced here: 73.5 us
  blocking collectives  46.4 us (63%)
  starting transfers between devices  14 us (19%)
  Pallas kernels  11.6 us (16%)
  between operations  0.83 us (1%)
    all_gather x1, blocking collectives, per_device(): got = lax.all_gather(packed, ROWS, axis=0, tiled=True)  27.5 us
    all_gather x1, blocking collectives, per_device(): mid = lax.all_gather(mid_half, ('x', 'c'), axis=0, tiled=True)  14.1 us
    ppermute x1, starting transfers between devices, per_device(): outer = lax.ppermute(solved, ALL, straight)  8.84 us
    ppermute x1, starting transfers between devices, per_device(): lax.ppermute(part, 'y', [(i, i ^ 1) for i in range(lax.axis_size('y'))])  3.21 us
    pallas_call x1, Pallas kernels, per_device(): call(ready_kernel, (tall, square, tall, square), [VMEM] * 7, 16 * W * W *...  2.77 us
    pallas_call x1, Pallas kernels, per_device(): call(leaf_kernel, shape(2, W, K), [SMEM] + [VMEM] * 6, 4 * W * W * K, 12...  2.57 us
    all_gather x1, blocking collectives, per_device(): chip = lax.all_gather(solved, 'c', axis=0, tiled=True)  2.37 us
    all_gather x1, blocking collectives, per_device(): nearby = lax.all_gather(inner, 'c', axis=0, tiled=True)  2.36 us
  transfers between devices with their start and end apart: 3, of which 0 were waited for; matrix products, arithmetic and copies ran while one was open for 0% of the time, Pallas kernels for 7%

profile of v3, /device:TPU:1, one launch (start us, length us, event | category | flops | bytes accessed | tf_op | source)
XLA Modules:
  0.0 73.5 jit_solution(746328778113675316)
XLA Ops:
  0.6 0.0 copy-start
  0.6 0.0 copy-start.1
  0.7 1.7 %shard_map.192 = (bf16[24,1280]{1,0:T(8,128)(2,1)}, s32[1,128]{1,0:T(1,128)}) custom-call(bf16[24,384]{1,0:T(8,128)(2,1)} %root_inverse.1, bf16[24,256]{1,0:T(8,128)(2,1)} %root_rhs.1, bf16[4,24,384]{2,1,0:T(8,128)(2,1)} %panels.4, bf16[4,24,384]{2,1,0:T(8,128)(2,1)} %inverses.2, bf16[4,24,256]{2,1,0:T(8,128)(2,1)} %rhs.3, s32[1024]{0:T(1024)} %bitcast.1, ...), custom_call_target="tpu_custom_call" | custom-call | bytes 122880 | tf_op jit(solution)/shard_map/pallas_call | solution.py:228
  2.4 0.0 copy-start.4
  2.4 27.5 %all_gather.12.got = bf16[384,1280]{1,0:T(8,128)(2,1)S(1)} all-gather(bf16[24,1280]{1,0:T(8,128)(2,1)} %get-tuple-element.22), channel_id=1, replica_groups=mesh['y'=8,'x'=4,'z'=8,'c'=2] {'z','c'}, dimensions={0}, use_global_device_ids=true | all-gather | bytes 1044480 | tf_op jit(solution)/shard_map/all_gather | solution.py:239
  29.9 0.0 copy-done
  29.9 0.0 copy-done.1
  29.9 0.0 copy-done.4
  29.9 0.0 copy-start.7
  29.9 0.0 copy-start.8
  29.9 0.0 copy-start.9
  30.0 1.1 %shard_map.193 = (bf16[384,256]{1,0:T(8,128)(2,1)S(1)}, bf16[192,256]{1,0:T(8,128)(2,1)S(1)}) custom-call(bf16[384,1280]{1,0:T(8,128)(2,1)S(1)} %all_gather.12.got, s32[4,384]{1,0:T(4,128)S(1)} %copy-done.4, bf16[2,384,384]{2,1,0:T(8,128)(2,1)S(1)} %copy-done.1, bf16[2,384,384]{2,1,0:T(8,128)(2,1)S(1)} %copy-done), custom_call_target="tpu_custom_call" | custom-call | flops 150994944 | bytes 983040 | tf_op jit(solution)/shard_map/pallas_call | solution.py:242
  31.0 0.0 copy-start.6
  31.0 3.2 %collective-permute-start = (bf16[192,256]{1,0:T(8,128)(2,1)S(1)}, bf16[192,256]{1,0:T(8,128)(2,1)S(1)}, u32[]{:S(2)}, u32[]{:S(2)}) collective-permute-start(bf16[192,256]{1,0:T(8,128)(2,1)S(1)} %get-tuple-element.24), channel_id=1, source_target_pairs={{0,64},{64,0},{128,192},{192,128},{256,320},{320,256},{384,448},{4... | collective-permute-start | bytes 294920 | tf_op jit(solution)/shard_map/ppermute | solution.py:249
  34.2 0.0 copy-start.5
  34.3 0.0 copy-done.7
  34.3 0.0 copy-done.8
  34.3 0.0 copy-done.9
  34.3 0.0 copy-done.6
  34.3 0.6 copy-done.5
  34.9 2.8 %shard_map.194 = (f32[2,384,256]{2,1,0:T(8,128)S(1)}, bf16[2,384,384]{2,1,0:T(8,128)(2,1)S(1)}, f32[2,384,256]{2,1,0:T(8,128)S(1)}, bf16[2,384,384]{2,1,0:T(8,128)(2,1)S(1)}) custom-call(s32[2,384]{1,0:T(2,128)S(1)} %copy-done.9, bf16[2,384,384]{2,1,0:T(8,128)(2,1)S(1)} %copy-done.7, bf16[2,384,256]{2,1,0:T(8,128)(2,1)S(1)} %copy-done.8, ...), custom_call_target="tpu_custom_call" | custom-call | flops 1207959552 | bytes 6291456 | tf_op jit(solution)/shard_map/pallas_call | solution.py:250
  37.7 0.0 copy-start.2
  37.7 0.0 collective-permute-done
  37.7 14.1 %all_gather.13.mid = bf16[1536,256]{1,0:T(8,128)(2,1)S(1)} all-gather(bf16[192,256]{1,0:T(8,128)(2,1)S(1)} %add_convert_fusion), channel_id=1, replica_groups=mesh['y'=8,'x'=4,'z'=8,'c'=2] {'x','c'}, dimensions={0}, use_global_device_ids=true | all-gather | bytes 884736 | tf_op jit(solution)/shard_map/all_gather | solution.py:259
  51.9 0.0 copy-done.2
  51.9 0.0 copy-start.3
  51.9 1.4 %shard_map.195.solved = bf16[2,384,256]{2,1,0:T(8,128)(2,1)S(1)} custom-call(s32[1,128]{1,0:T(1,128)S(1)} %copy-done.5, bf16[1536,256]{1,0:T(8,128)(2,1)S(1)} %all_gather.13.mid, f32[2,384,256]{2,1,0:T(8,128)S(1)} %get-tuple-element.27.base, bf16[2,384,384]{2,1,0:T(8,128)(2,1)S(1)} %get-tuple-element.28.spread, bf16[2,384,384]{2,1,0:T(8,128)(2,1)S(1)} %copy-done.2), custom_call_target="tpu_custom_call" | custom-call | flops 301989888 | bytes 3342336 | tf_op jit(solution)/shard_map/pallas_call | solution.py:260
  53.3 1.9 %collective-permute-start.1 = (bf16[2,384,256]{2,1,0:T(8,128)(2,1)S(1)}, bf16[2,384,256]{2,1,0:T(8,128)(2,1)S(1)}, u32[]{:S(2)}, u32[]{:S(2)}) collective-permute-start(bf16[2,384,256]{2,1,0:T(8,128)(2,1)S(1)} %shard_map.195.solved), channel_id=1, source_target_pairs={{511,0},{1,2},{3,4},{5,6},{7,8},{9,10},{11,12},{13,14},{15,16},{17... | collective-permute-start | bytes 1179656 | tf_op jit(solution)/shard_map/ppermute | solution.py:272
  55.2 8.8 %collective-permute-start.2 = (bf16[2,384,256]{2,1,0:T(8,128)(2,1)S(1)}, bf16[2,384,256]{2,1,0:T(8,128)(2,1)S(1)}, u32[]{:S(2)}, u32[]{:S(2)}) collective-permute-start(bf16[2,384,256]{2,1,0:T(8,128)(2,1)S(1)} %shard_map.195.solved), channel_id=1, source_target_pairs={{510,0},{0,2},{2,4},{4,6},{6,8},{8,10},{10,12},{12,14},{14,16},{16... | collective-permute-start | bytes 1179656 | tf_op jit(solution)/shard_map/ppermute | solution.py:273
  64.1 0.0 copy-done.3
  64.1 2.1 %shard_map.196 = (f32[2,384,256]{2,1,0:T(8,128)S(1)}, bf16[24,256]{1,0:T(8,128)(2,1)}, bf16[4,24,256]{2,1,0:T(8,128)(2,1)}, bf16[2,384,256]{2,1,0:T(8,128)(2,1)}) custom-call(s32[1,128]{1,0:T(1,128)S(1)} %copy-done.5, s32[2,384]{1,0:T(2,128)S(1)} %copy-done.6, bf16[2,384,384]{2,1,0:T(8,128)(2,1)S(1)} %copy-done.1, bf16[2,384,256]{2,1,0:T(8,128)(2,1)S(1)} %copy-done.3, ...), custom_call_target="tpu_custom_call" | custom-call | flops 301989888 | bytes 3538944 | tf_op jit(solution)/shard_map/pallas_call | solution.py:275
  66.2 2.4 %all_gather.14.chip = bf16[4,384,256]{2,1,0:T(8,128)(2,1)S(1)} all-gather(bf16[2,384,256]{2,1,0:T(8,128)(2,1)S(1)} %shard_map.195.solved), channel_id=1, replica_groups=mesh['y'=8,'x'=4,'z'=8,'c'=2] {'c'}, dimensions={0}, use_global_device_ids=true | all-gather | bytes 1179648 | tf_op jit(solution)/shard_map/all_gather | solution.py:274
  68.5 0.0 collective-permute-done.1
  68.6 2.4 %all_gather.15.nearby = bf16[4,384,256]{2,1,0:T(8,128)(2,1)S(1)} all-gather(bf16[2,384,256]{2,1,0:T(8,128)(2,1)S(1)} %collective-permute-done.1), channel_id=1, replica_groups=mesh['y'=8,'x'=4,'z'=8,'c'=2] {'c'}, dimensions={0}, use_global_device_ids=true | all-gather | bytes 1179648 | tf_op jit(solution)/shard_map/all_gather | solution.py:285
  70.9 0.0 collective-permute-done.2.outer
  70.9 2.6 %shard_map.197 = bf16[2,384,256]{2,1,0:T(8,128)(2,1)} custom-call(s32[1,128]{1,0:T(1,128)S(1)} %copy-done.5, f32[2,384,256]{2,1,0:T(8,128)S(1)} %get-tuple-element.34.base, bf16[2,384,384]{2,1,0:T(8,128)(2,1)S(1)} %get-tuple-element.35.spread, bf16[2,384,384]{2,1,0:T(8,128)(2,1)S(1)} %copy-done, bf16[4,384,256]{2,1,0:T(8,128)(2,1)S(1)} %all_gather.14.chip, ...), custom_call_target="tpu_custom_call" | custom-call | flops 301989888 | bytes 4128768 | tf_op jit(solution)/shard_map/pallas_call | solution.py:286
  (1 shorter events, 0.0 us)
Async XLA Ops:
  0.6 29.3 %copy-start = (bf16[2,384,384]{2,1,0:T(8,128)(2,1)S(1)}, bf16[2,384,384]{2,1,0:T(8,128)(2,1)}, u32[]{:S(2)}) copy-start(bf16[2,384,384]{2,1,0:T(8,128)(2,1)} %inverse.3) | copy-start | bytes 1769476
  0.6 29.3 %copy-start.1 = (bf16[2,384,384]{2,1,0:T(8,128)(2,1)S(1)}, bf16[2,384,384]{2,1,0:T(8,128)(2,1)}, u32[]{:S(2)}) copy-start(bf16[2,384,384]{2,1,0:T(8,128)(2,1)} %panels.7) | copy-start | bytes 1769476
  2.4 27.5 %copy-start.4 = (s32[4,384]{1,0:T(4,128)S(1)}, s32[4,384]{1,0:T(4,128)}, u32[]{:S(2)}) copy-start(s32[4,384]{1,0:T(4,128)} %mid_rows.1) | copy-start | bytes 18436
  29.9 4.3 %copy-start.7 = (bf16[2,384,384]{2,1,0:T(8,128)(2,1)S(1)}, bf16[2,384,384]{2,1,0:T(8,128)(2,1)}, u32[]{:S(2)}) copy-start(bf16[2,384,384]{2,1,0:T(8,128)(2,1)} %panels.6) | copy-start | bytes 1769476
  29.9 4.3 %copy-start.8 = (bf16[2,384,256]{2,1,0:T(8,128)(2,1)S(1)}, bf16[2,384,256]{2,1,0:T(8,128)(2,1)}, u32[]{:S(2)}) copy-start(bf16[2,384,256]{2,1,0:T(8,128)(2,1)} %rhs.4) | copy-start | bytes 1179652
  29.9 4.3 %copy-start.9 = (s32[2,384]{1,0:T(2,128)S(1)}, s32[2,384]{1,0:T(2,128)}, u32[]{:S(2)}) copy-start(s32[2,384]{1,0:T(2,128)} %rows.2) | copy-start | bytes 9220
  31.0 3.3 %copy-start.6 = (s32[2,384]{1,0:T(2,128)S(1)}, s32[2,384]{1,0:T(2,128)}, u32[]{:S(2)}) copy-start(s32[2,384]{1,0:T(2,128)} %rows.3) | copy-start | bytes 9220
  31.0 6.7 %collective-permute-start = (bf16[192,256]{1,0:T(8,128)(2,1)S(1)}, bf16[192,256]{1,0:T(8,128)(2,1)S(1)}, u32[]{:S(2)}, u32[]{:S(2)}) collective-permute-start(bf16[192,256]{1,0:T(8,128)(2,1)S(1)} %get-tuple-element.24), channel_id=1, source_target_pairs={{0,64},{64,0},{128,192},{192,128},{256,320},{320,256},{384,448},{4... | collective-permute-start | bytes 294920 | tf_op jit(solution)/shard_map/ppermute | solution.py:249
  34.2 0.7 copy-start.5
  37.7 14.2 %copy-start.2 = (bf16[2,384,384]{2,1,0:T(8,128)(2,1)S(1)}, bf16[2,384,384]{2,1,0:T(8,128)(2,1)}, u32[]{:S(2)}) copy-start(bf16[2,384,384]{2,1,0:T(8,128)(2,1)} %inverse.2) | copy-start | bytes 1769476
  51.9 12.2 %copy-start.3 = (bf16[2,384,256]{2,1,0:T(8,128)(2,1)S(1)}, bf16[2,384,256]{2,1,0:T(8,128)(2,1)}, u32[]{:S(2)}) copy-start(bf16[2,384,256]{2,1,0:T(8,128)(2,1)} %rhs.5) | copy-start | bytes 1179652
  53.3 15.3 %collective-permute-start.1 = (bf16[2,384,256]{2,1,0:T(8,128)(2,1)S(1)}, bf16[2,384,256]{2,1,0:T(8,128)(2,1)S(1)}, u32[]{:S(2)}, u32[]{:S(2)}) collective-permute-start(bf16[2,384,256]{2,1,0:T(8,128)(2,1)S(1)} %shard_map.195.solved), channel_id=1, source_target_pairs={{511,0},{1,2},{3,4},{5,6},{7,8},{9,10},{11,12},{13,14},{15,16},{17... | collective-permute-start | bytes 1179656 | tf_op jit(solution)/shard_map/ppermute | solution.py:272
  55.2 15.7 %collective-permute-start.2 = (bf16[2,384,256]{2,1,0:T(8,128)(2,1)S(1)}, bf16[2,384,256]{2,1,0:T(8,128)(2,1)S(1)}, u32[]{:S(2)}, u32[]{:S(2)}) collective-permute-start(bf16[2,384,256]{2,1,0:T(8,128)(2,1)S(1)} %shard_map.195.solved), channel_id=1, source_target_pairs={{510,0},{0,2},{2,4},{4,6},{6,8},{8,10},{10,12},{12,14},{14,16},{16... | collective-permute-start | bytes 1179656 | tf_op jit(solution)/shard_map/ppermute | solution.py:273

commit v4 on v3

--- a/solution.py
+++ b/solution.py
@@ -150,9 +150,11 @@
 
 
 def sub_kernel(facts, mid, base, spread, inverse, out):
-    for n in range(2):
-        update = (base[n] - dot(spread[n], rows_of(mid, facts[0, 5 * n]))).astype(BF16)
-        out[n] = dot(inverse[n], update).astype(BF16)
+    updates = [
+        (base[n] - dot(spread[n], rows_of(mid, facts[0, 5 * n]))).astype(BF16) for n in range(2)
+    ]
+    for n in range(2):
+        out[n] = dot(inverse[n], updates[n]).astype(BF16)
 
 
 def leaf_middle_kernel(
@@ -177,9 +179,8 @@
 
 
 def leaf_kernel(facts, base, spread, inverse, chip, nearby, outer, out, held, done, sems):
-    stores = []
-    for n in range(2):
-        block, member, live = (facts[0, 5 * n + i] for i in (2, 3, 4))
+    for n in range(2):
+        block, member = facts[0, 5 * n + 2], facts[0, 5 * n + 3]
 
         @pl.when(jnp.logical_or(block == 0, block == 1))
         def _():
@@ -193,10 +194,12 @@
         def _():
             held[n] = outer[member]
 
-        update = (base[n] - dot(spread[n], held[n])).astype(BF16)
-        solved = dot(inverse[n], update)
-        row = lax.broadcasted_iota(jnp.int32, (W, K), 0)
-        done[n] = jnp.where(row < live, solved, 0.0).astype(BF16)
+    row = lax.broadcasted_iota(jnp.int32, (W, K), 0)
+    updates = [(base[n] - dot(spread[n], held[n])).astype(BF16) for n in range(2)]
+    stores = []
+    for n in range(2):
+        solved = dot(inverse[n], updates[n])
+        done[n] = jnp.where(row < facts[0, 5 * n + 4], solved, 0.0).astype(BF16)
         stores.append(pltpu.make_async_copy(done.at[n], out.at[n], sems.at[n]))
         stores[n].start()
     for store in stores:

time: 73.8 us -> 73.1 us (level)
  no operation moved by 1% of the time
where the time goes in v4:
time: 73.1 us; the launch traced here: 72.8 us
  blocking collectives  46.4 us (63%)
  starting transfers between devices  14 us (19%)
  Pallas kernels  10.9 us (15%)
  between operations  0.83 us (1%)
    all_gather x1, blocking collectives, per_device(): got = lax.all_gather(packed, ROWS, axis=0, tiled=True)  27.5 us
    all_gather x1, blocking collectives, per_device(): mid = lax.all_gather(mid_half, ('x', 'c'), axis=0, tiled=True)  14.1 us
    ppermute x1, starting transfers between devices, per_device(): outer = lax.ppermute(solved, ALL, straight)  8.84 us
    ppermute x1, starting transfers between devices, per_device(): lax.ppermute(part, 'y', [(i, i ^ 1) for i in range(lax.axis_size('y'))])  3.21 us
    pallas_call x1, Pallas kernels, per_device(): call(ready_kernel, (tall, square, tall, square), [VMEM] * 7, 16 * W * W *...  2.77 us
    all_gather x1, blocking collectives, per_device(): chip = lax.all_gather(solved, 'c', axis=0, tiled=True)  2.37 us
    all_gather x1, blocking collectives, per_device(): nearby = lax.all_gather(inner, 'c', axis=0, tiled=True)  2.36 us
    pallas_call x1, Pallas kernels, per_device(): call(leaf_middle_kernel, (tall, shape(own_rows, K), shape(mid_rows.shape[...  2.11 us
  transfers between devices with their start and end apart: 3, of which 0 were waited for; matrix products, arithmetic and copies ran while one was open for 0% of the time, Pallas kernels for 7%

profile of v4, /device:TPU:1, one launch (start us, length us, event | category | flops | bytes accessed | tf_op | source)
XLA Modules:
  0.0 72.8 jit_solution(8317873437793664044)
XLA Ops:
  0.6 0.0 copy-start
  0.6 0.0 copy-start.1
  0.7 1.7 %shard_map.192 = (bf16[24,1280]{1,0:T(8,128)(2,1)}, s32[1,128]{1,0:T(1,128)}) custom-call(bf16[24,384]{1,0:T(8,128)(2,1)} %root_inverse.1, bf16[24,256]{1,0:T(8,128)(2,1)} %root_rhs.1, bf16[4,24,384]{2,1,0:T(8,128)(2,1)} %panels.4, bf16[4,24,384]{2,1,0:T(8,128)(2,1)} %inverses.2, bf16[4,24,256]{2,1,0:T(8,128)(2,1)} %rhs.3, s32[1024]{0:T(1024)} %bitcast.1, ...), custom_call_target="tpu_custom_call" | custom-call | bytes 122880 | tf_op jit(solution)/shard_map/pallas_call | solution.py:231
  2.4 0.0 copy-start.4
  2.4 27.5 %all_gather.12.got = bf16[384,1280]{1,0:T(8,128)(2,1)S(1)} all-gather(bf16[24,1280]{1,0:T(8,128)(2,1)} %get-tuple-element.22), channel_id=1, replica_groups=mesh['y'=8,'x'=4,'z'=8,'c'=2] {'z','c'}, dimensions={0}, use_global_device_ids=true | all-gather | bytes 1044480 | tf_op jit(solution)/shard_map/all_gather | solution.py:242
  29.9 0.0 copy-done
  29.9 0.0 copy-done.1
  29.9 0.0 copy-done.4
  29.9 0.0 copy-start.7
  29.9 0.0 copy-start.8
  29.9 0.0 copy-start.9
  30.0 1.1 %shard_map.193 = (bf16[384,256]{1,0:T(8,128)(2,1)S(1)}, bf16[192,256]{1,0:T(8,128)(2,1)S(1)}) custom-call(bf16[384,1280]{1,0:T(8,128)(2,1)S(1)} %all_gather.12.got, s32[4,384]{1,0:T(4,128)S(1)} %copy-done.4, bf16[2,384,384]{2,1,0:T(8,128)(2,1)S(1)} %copy-done.1, bf16[2,384,384]{2,1,0:T(8,128)(2,1)S(1)} %copy-done), custom_call_target="tpu_custom_call" | custom-call | flops 150994944 | bytes 983040 | tf_op jit(solution)/shard_map/pallas_call | solution.py:245
  31.0 0.0 copy-start.6
  31.0 3.2 %collective-permute-start = (bf16[192,256]{1,0:T(8,128)(2,1)S(1)}, bf16[192,256]{1,0:T(8,128)(2,1)S(1)}, u32[]{:S(2)}, u32[]{:S(2)}) collective-permute-start(bf16[192,256]{1,0:T(8,128)(2,1)S(1)} %get-tuple-element.24), channel_id=1, source_target_pairs={{0,64},{64,0},{128,192},{192,128},{256,320},{320,256},{384,448},{4... | collective-permute-start | bytes 294920 | tf_op jit(solution)/shard_map/ppermute | solution.py:252
  34.2 0.0 copy-start.5
  34.3 0.0 copy-done.7
  34.3 0.0 copy-done.8
  34.3 0.0 copy-done.9
  34.3 0.0 copy-done.6
  34.3 0.6 copy-done.5
  34.9 2.8 %shard_map.194 = (f32[2,384,256]{2,1,0:T(8,128)S(1)}, bf16[2,384,384]{2,1,0:T(8,128)(2,1)S(1)}, f32[2,384,256]{2,1,0:T(8,128)S(1)}, bf16[2,384,384]{2,1,0:T(8,128)(2,1)S(1)}) custom-call(s32[2,384]{1,0:T(2,128)S(1)} %copy-done.9, bf16[2,384,384]{2,1,0:T(8,128)(2,1)S(1)} %copy-done.7, bf16[2,384,256]{2,1,0:T(8,128)(2,1)S(1)} %copy-done.8, ...), custom_call_target="tpu_custom_call" | custom-call | flops 1207959552 | bytes 6291456 | tf_op jit(solution)/shard_map/pallas_call | solution.py:253
  37.7 0.0 copy-start.2
  37.7 0.0 collective-permute-done
  37.7 14.1 %all_gather.13.mid = bf16[1536,256]{1,0:T(8,128)(2,1)S(1)} all-gather(bf16[192,256]{1,0:T(8,128)(2,1)S(1)} %add_convert_fusion), channel_id=1, replica_groups=mesh['y'=8,'x'=4,'z'=8,'c'=2] {'x','c'}, dimensions={0}, use_global_device_ids=true | all-gather | bytes 884736 | tf_op jit(solution)/shard_map/all_gather | solution.py:262
  51.9 0.0 copy-done.2
  51.9 0.0 copy-start.3
  51.9 1.2 %shard_map.195.solved = bf16[2,384,256]{2,1,0:T(8,128)(2,1)S(1)} custom-call(s32[1,128]{1,0:T(1,128)S(1)} %copy-done.5, bf16[1536,256]{1,0:T(8,128)(2,1)S(1)} %all_gather.13.mid, f32[2,384,256]{2,1,0:T(8,128)S(1)} %get-tuple-element.27.base, bf16[2,384,384]{2,1,0:T(8,128)(2,1)S(1)} %get-tuple-element.28.spread, bf16[2,384,384]{2,1,0:T(8,128)(2,1)S(1)} %copy-done.2), custom_call_target="tpu_custom_call" | custom-call | flops 301989888 | bytes 3342336 | tf_op jit(solution)/shard_map/pallas_call | solution.py:263
  53.1 1.9 %collective-permute-start.1 = (bf16[2,384,256]{2,1,0:T(8,128)(2,1)S(1)}, bf16[2,384,256]{2,1,0:T(8,128)(2,1)S(1)}, u32[]{:S(2)}, u32[]{:S(2)}) collective-permute-start(bf16[2,384,256]{2,1,0:T(8,128)(2,1)S(1)} %shard_map.195.solved), channel_id=1, source_target_pairs={{511,0},{1,2},{3,4},{5,6},{7,8},{9,10},{11,12},{13,14},{15,16},{17... | collective-permute-start | bytes 1179656 | tf_op jit(solution)/shard_map/ppermute | solution.py:275
  55.0 8.8 %collective-permute-start.2 = (bf16[2,384,256]{2,1,0:T(8,128)(2,1)S(1)}, bf16[2,384,256]{2,1,0:T(8,128)(2,1)S(1)}, u32[]{:S(2)}, u32[]{:S(2)}) collective-permute-start(bf16[2,384,256]{2,1,0:T(8,128)(2,1)S(1)} %shard_map.195.solved), channel_id=1, source_target_pairs={{510,0},{0,2},{2,4},{4,6},{6,8},{8,10},{10,12},{12,14},{14,16},{16... | collective-permute-start | bytes 1179656 | tf_op jit(solution)/shard_map/ppermute | solution.py:276
  63.9 0.0 copy-done.3
  63.9 2.1 %shard_map.196 = (f32[2,384,256]{2,1,0:T(8,128)S(1)}, bf16[24,256]{1,0:T(8,128)(2,1)}, bf16[4,24,256]{2,1,0:T(8,128)(2,1)}, bf16[2,384,256]{2,1,0:T(8,128)(2,1)}) custom-call(s32[1,128]{1,0:T(1,128)S(1)} %copy-done.5, s32[2,384]{1,0:T(2,128)S(1)} %copy-done.6, bf16[2,384,384]{2,1,0:T(8,128)(2,1)S(1)} %copy-done.1, bf16[2,384,256]{2,1,0:T(8,128)(2,1)S(1)} %copy-done.3, ...), custom_call_target="tpu_custom_call" | custom-call | flops 301989888 | bytes 3538944 | tf_op jit(solution)/shard_map/pallas_call | solution.py:278
  66.0 2.4 %all_gather.14.chip = bf16[4,384,256]{2,1,0:T(8,128)(2,1)S(1)} all-gather(bf16[2,384,256]{2,1,0:T(8,128)(2,1)S(1)} %shard_map.195.solved), channel_id=1, replica_groups=mesh['y'=8,'x'=4,'z'=8,'c'=2] {'c'}, dimensions={0}, use_global_device_ids=true | all-gather | bytes 1179648 | tf_op jit(solution)/shard_map/all_gather | solution.py:277
  68.4 0.0 collective-permute-done.1
  68.4 2.4 %all_gather.15.nearby = bf16[4,384,256]{2,1,0:T(8,128)(2,1)S(1)} all-gather(bf16[2,384,256]{2,1,0:T(8,128)(2,1)S(1)} %collective-permute-done.1), channel_id=1, replica_groups=mesh['y'=8,'x'=4,'z'=8,'c'=2] {'c'}, dimensions={0}, use_global_device_ids=true | all-gather | bytes 1179648 | tf_op jit(solution)/shard_map/all_gather | solution.py:288
  70.7 0.0 collective-permute-done.2.outer
  70.7 2.0 %shard_map.197 = bf16[2,384,256]{2,1,0:T(8,128)(2,1)} custom-call(s32[1,128]{1,0:T(1,128)S(1)} %copy-done.5, f32[2,384,256]{2,1,0:T(8,128)S(1)} %get-tuple-element.34.base, bf16[2,384,384]{2,1,0:T(8,128)(2,1)S(1)} %get-tuple-element.35.spread, bf16[2,384,384]{2,1,0:T(8,128)(2,1)S(1)} %copy-done, bf16[4,384,256]{2,1,0:T(8,128)(2,1)S(1)} %all_gather.14.chip, ...), custom_call_target="tpu_custom_call" | custom-call | flops 301989888 | bytes 4128768 | tf_op jit(solution)/shard_map/pallas_call | solution.py:289
  (1 shorter events, 0.0 us)
Async XLA Ops:
  0.6 29.3 %copy-start = (bf16[2,384,384]{2,1,0:T(8,128)(2,1)S(1)}, bf16[2,384,384]{2,1,0:T(8,128)(2,1)}, u32[]{:S(2)}) copy-start(bf16[2,384,384]{2,1,0:T(8,128)(2,1)} %inverse.3) | copy-start | bytes 1769476
  0.6 29.3 %copy-start.1 = (bf16[2,384,384]{2,1,0:T(8,128)(2,1)S(1)}, bf16[2,384,384]{2,1,0:T(8,128)(2,1)}, u32[]{:S(2)}) copy-start(bf16[2,384,384]{2,1,0:T(8,128)(2,1)} %panels.7) | copy-start | bytes 1769476
  2.4 27.5 %copy-start.4 = (s32[4,384]{1,0:T(4,128)S(1)}, s32[4,384]{1,0:T(4,128)}, u32[]{:S(2)}) copy-start(s32[4,384]{1,0:T(4,128)} %mid_rows.1) | copy-start | bytes 18436
  29.9 4.3 %copy-start.7 = (bf16[2,384,384]{2,1,0:T(8,128)(2,1)S(1)}, bf16[2,384,384]{2,1,0:T(8,128)(2,1)}, u32[]{:S(2)}) copy-start(bf16[2,384,384]{2,1,0:T(8,128)(2,1)} %panels.6) | copy-start | bytes 1769476
  29.9 4.3 %copy-start.8 = (bf16[2,384,256]{2,1,0:T(8,128)(2,1)S(1)}, bf16[2,384,256]{2,1,0:T(8,128)(2,1)}, u32[]{:S(2)}) copy-start(bf16[2,384,256]{2,1,0:T(8,128)(2,1)} %rhs.4) | copy-start | bytes 1179652
  29.9 4.3 %copy-start.9 = (s32[2,384]{1,0:T(2,128)S(1)}, s32[2,384]{1,0:T(2,128)}, u32[]{:S(2)}) copy-start(s32[2,384]{1,0:T(2,128)} %rows.2) | copy-start | bytes 9220
  31.0 3.3 %copy-start.6 = (s32[2,384]{1,0:T(2,128)S(1)}, s32[2,384]{1,0:T(2,128)}, u32[]{:S(2)}) copy-start(s32[2,384]{1,0:T(2,128)} %rows.3) | copy-start | bytes 9220
  31.0 6.7 %collective-permute-start = (bf16[192,256]{1,0:T(8,128)(2,1)S(1)}, bf16[192,256]{1,0:T(8,128)(2,1)S(1)}, u32[]{:S(2)}, u32[]{:S(2)}) collective-permute-start(bf16[192,256]{1,0:T(8,128)(2,1)S(1)} %get-tuple-element.24), channel_id=1, source_target_pairs={{0,64},{64,0},{128,192},{192,128},{256,320},{320,256},{384,448},{4... | collective-permute-start | bytes 294920 | tf_op jit(solution)/shard_map/ppermute | solution.py:252
  34.2 0.7 copy-start.5
  37.7 14.2 %copy-start.2 = (bf16[2,384,384]{2,1,0:T(8,128)(2,1)S(1)}, bf16[2,384,384]{2,1,0:T(8,128)(2,1)}, u32[]{:S(2)}) copy-start(bf16[2,384,384]{2,1,0:T(8,128)(2,1)} %inverse.2) | copy-start | bytes 1769476
  51.9 12.0 %copy-start.3 = (bf16[2,384,256]{2,1,0:T(8,128)(2,1)S(1)}, bf16[2,384,256]{2,1,0:T(8,128)(2,1)}, u32[]{:S(2)}) copy-start(bf16[2,384,256]{2,1,0:T(8,128)(2,1)} %rhs.5) | copy-start | bytes 1179652
  53.1 15.3 %collective-permute-start.1 = (bf16[2,384,256]{2,1,0:T(8,128)(2,1)S(1)}, bf16[2,384,256]{2,1,0:T(8,128)(2,1)S(1)}, u32[]{:S(2)}, u32[]{:S(2)}) collective-permute-start(bf16[2,384,256]{2,1,0:T(8,128)(2,1)S(1)} %shard_map.195.solved), channel_id=1, source_target_pairs={{511,0},{1,2},{3,4},{5,6},{7,8},{9,10},{11,12},{13,14},{15,16},{17... | collective-permute-start | bytes 1179656 | tf_op jit(solution)/shard_map/ppermute | solution.py:275
  55.0 15.7 %collective-permute-start.2 = (bf16[2,384,256]{2,1,0:T(8,128)(2,1)S(1)}, bf16[2,384,256]{2,1,0:T(8,128)(2,1)S(1)}, u32[]{:S(2)}, u32[]{:S(2)}) collective-permute-start(bf16[2,384,256]{2,1,0:T(8,128)(2,1)S(1)} %shard_map.195.solved), channel_id=1, source_target_pairs={{510,0},{0,2},{2,4},{4,6},{6,8},{8,10},{10,12},{12,14},{14,16},{16... | collective-permute-start | bytes 1179656 | tf_op jit(solution)/shard_map/ppermute | solution.py:276

commit v5 on v4

--- a/solution.py
+++ b/solution.py
@@ -145,13 +145,18 @@
         low_spread[n] = dot(turned, one_hot(index, 2 * W, W // LANE)).astype(BF16)
 
 
+def fact(facts, place):
+    lane = lax.broadcasted_iota(jnp.int32, facts.shape, 1)
+    return jnp.sum(jnp.where(lane == place, facts[...], 0))
+
+
 def rows_of(mid, parent):
     return mid[pl.ds(pl.multiple_of(parent * W, W), W), :]
 
 
 def sub_kernel(facts, mid, base, spread, inverse, out):
     updates = [
-        (base[n] - dot(spread[n], rows_of(mid, facts[0, 5 * n]))).astype(BF16) for n in range(2)
+        (base[n] - dot(spread[n], rows_of(mid, fact(facts, 5 * n)))).astype(BF16) for n in range(2)
     ]
     for n in range(2):
         out[n] = dot(inverse[n], updates[n]).astype(BF16)
@@ -172,7 +177,7 @@
         mid_own[s] = dot(own, mid[s * W : (s + 1) * W, :]).astype(BF16)
     for n in range(2):
         index = rows[n : n + 1, :]
-        above = rows_of(mid, facts[0, 5 * n + 1])
+        above = rows_of(mid, fact(facts, 5 * n + 1))
         picked = dot(one_hot(index, W, W // LANE), above).astype(BF16)
         base[n] = rhs[n].astype(F32) - from_root[n] - dot(panels[n].T, picked)
     store.wait()
@@ -180,7 +185,7 @@
 
 def leaf_kernel(facts, base, spread, inverse, chip, nearby, outer, out, held, done, sems):
     for n in range(2):
-        block, member = facts[0, 5 * n + 2], facts[0, 5 * n + 3]
+        block, member = fact(facts, 5 * n + 2), fact(facts, 5 * n + 3)
 
         @pl.when(jnp.logical_or(block == 0, block == 1))
         def _():
@@ -199,7 +204,7 @@
     stores = []
     for n in range(2):
         solved = dot(inverse[n], updates[n])
-        done[n] = jnp.where(row < facts[0, 5 * n + 4], solved, 0.0).astype(BF16)
+        done[n] = jnp.where(row < fact(facts, 5 * n + 4), solved, 0.0).astype(BF16)
         stores.append(pltpu.make_async_copy(done.at[n], out.at[n], sems.at[n]))
         stores[n].start()
     for store in stores:
@@ -263,7 +268,7 @@
     solved = call(
         sub_kernel,
         shape(2, W, K),
-        [SMEM] + [VMEM] * 4,
+        [VMEM] * 5,
         4 * W * W * K,
         12 * W * W + 16 * W * K,
     )(facts, mid, base, spread, sub_inverse)
@@ -278,7 +283,7 @@
     leaf_base, root_own, mid_own, sub_solution = call(
         leaf_middle_kernel,
         (tall, shape(own_rows, K), shape(mid_rows.shape[0], own_rows, K), thin),
-        [SMEM] + [VMEM] * 7,
+        [VMEM] * 8,
         4 * W * W * K,
         8 * W * W + 24 * W * K,
         places=(VMEM,) * 3 + (HBM,),
@@ -289,7 +294,7 @@
     leaf_solution = call(
         leaf_kernel,
         shape(2, W, K),
-        [SMEM] + [VMEM] * 6,
+        [VMEM] * 7,
         4 * W * W * K,
         12 * W * W + 24 * W * K,
         places=HBM,

time: 73.1 us -> 72 us (0.985)
  Pallas kernels: 10.9 us -> 9.72 us
  transfers between devices with their start and end apart: 3 -> 3, of which waited for: 0 -> 0; matrix products, arithmetic and copies ran while one was open for 0% -> 0% of each run, Pallas kernels for 7% -> 6%
where the time goes in v5:
time: 72 us; the launch traced here: 71.6 us
  blocking collectives  46.4 us (64%)
  starting transfers between devices  14 us (19%)
  Pallas kernels  9.72 us (14%)
  between operations  0.83 us (1%)
    all_gather x1, blocking collectives, per_device(): got = lax.all_gather(packed, ROWS, axis=0, tiled=True)  27.5 us
    all_gather x1, blocking collectives, per_device(): mid = lax.all_gather(mid_half, ('x', 'c'), axis=0, tiled=True)  14.1 us
    ppermute x1, starting transfers between devices, per_device(): outer = lax.ppermute(solved, ALL, straight)  8.84 us
    ppermute x1, starting transfers between devices, per_device(): lax.ppermute(part, 'y', [(i, i ^ 1) for i in range(lax.axis_size('y'))])  3.21 us
    pallas_call x1, Pallas kernels, per_device(): call(ready_kernel, (tall, square, tall, square), [VMEM] * 7, 16 * W * W *...  2.77 us
    all_gather x1, blocking collectives, per_device(): chip = lax.all_gather(solved, 'c', axis=0, tiled=True)  2.37 us
    all_gather x1, blocking collectives, per_device(): nearby = lax.all_gather(inner, 'c', axis=0, tiled=True)  2.36 us
    ppermute x1, starting transfers between devices, per_device(): inner = lax.ppermute(solved, ALL, cross)  1.92 us
  transfers between devices with their start and end apart: 3, of which 0 were waited for; matrix products, arithmetic and copies ran while one was open for 0% of the time, Pallas kernels for 6%

profile of v5, /device:TPU:1, one launch (start us, length us, event | category | flops | bytes accessed | tf_op | source)
XLA Modules:
  0.0 71.6 jit_solution(16271907341487179449)
XLA Ops:
  0.6 0.0 copy-start
  0.6 0.0 copy-start.1
  0.7 1.7 %shard_map.192 = (bf16[24,1280]{1,0:T(8,128)(2,1)}, s32[1,128]{1,0:T(1,128)}) custom-call(bf16[24,384]{1,0:T(8,128)(2,1)} %root_inverse.1, bf16[24,256]{1,0:T(8,128)(2,1)} %root_rhs.1, bf16[4,24,384]{2,1,0:T(8,128)(2,1)} %panels.4, bf16[4,24,384]{2,1,0:T(8,128)(2,1)} %inverses.2, bf16[4,24,256]{2,1,0:T(8,128)(2,1)} %rhs.3, s32[1024]{0:T(1024)} %bitcast.1, ...), custom_call_target="tpu_custom_call" | custom-call | bytes 122880 | tf_op jit(solution)/shard_map/pallas_call | solution.py:236
  2.4 0.0 copy-start.4
  2.4 27.5 %all_gather.12.got = bf16[384,1280]{1,0:T(8,128)(2,1)S(1)} all-gather(bf16[24,1280]{1,0:T(8,128)(2,1)} %get-tuple-element.22), channel_id=1, replica_groups=mesh['y'=8,'x'=4,'z'=8,'c'=2] {'z','c'}, dimensions={0}, use_global_device_ids=true | all-gather | bytes 1044480 | tf_op jit(solution)/shard_map/all_gather | solution.py:247
  29.9 0.0 copy-done
  29.9 0.0 copy-done.1
  29.9 0.0 copy-done.4
  29.9 0.0 copy-start.7
  29.9 0.0 copy-start.8
  29.9 0.0 copy-start.9
  30.0 1.1 %shard_map.193 = (bf16[384,256]{1,0:T(8,128)(2,1)S(1)}, bf16[192,256]{1,0:T(8,128)(2,1)S(1)}) custom-call(bf16[384,1280]{1,0:T(8,128)(2,1)S(1)} %all_gather.12.got, s32[4,384]{1,0:T(4,128)S(1)} %copy-done.4, bf16[2,384,384]{2,1,0:T(8,128)(2,1)S(1)} %copy-done.1, bf16[2,384,384]{2,1,0:T(8,128)(2,1)S(1)} %copy-done), custom_call_target="tpu_custom_call" | custom-call | flops 150994944 | bytes 983040 | tf_op jit(solution)/shard_map/pallas_call | solution.py:250
  31.0 0.0 copy-start.6
  31.0 3.2 %collective-permute-start = (bf16[192,256]{1,0:T(8,128)(2,1)S(1)}, bf16[192,256]{1,0:T(8,128)(2,1)S(1)}, u32[]{:S(2)}, u32[]{:S(2)}) collective-permute-start(bf16[192,256]{1,0:T(8,128)(2,1)S(1)} %get-tuple-element.24), channel_id=1, source_target_pairs={{0,64},{64,0},{128,192},{192,128},{256,320},{320,256},{384,448},{4... | collective-permute-start | bytes 294920 | tf_op jit(solution)/shard_map/ppermute | solution.py:257
  34.2 0.0 copy-start.5
  34.3 0.0 copy-done.7
  34.3 0.0 copy-done.8
  34.3 0.0 copy-done.9
  34.3 0.0 copy-done.6
  34.3 0.6 copy-done.5
  34.9 2.8 %shard_map.194 = (f32[2,384,256]{2,1,0:T(8,128)S(1)}, bf16[2,384,384]{2,1,0:T(8,128)(2,1)S(1)}, f32[2,384,256]{2,1,0:T(8,128)S(1)}, bf16[2,384,384]{2,1,0:T(8,128)(2,1)S(1)}) custom-call(s32[2,384]{1,0:T(2,128)S(1)} %copy-done.9, bf16[2,384,384]{2,1,0:T(8,128)(2,1)S(1)} %copy-done.7, bf16[2,384,256]{2,1,0:T(8,128)(2,1)S(1)} %copy-done.8, ...), custom_call_target="tpu_custom_call" | custom-call | flops 1207959552 | bytes 6291456 | tf_op jit(solution)/shard_map/pallas_call | solution.py:258
  37.7 0.0 copy-start.2
  37.7 0.0 collective-permute-done
  37.7 14.1 %all_gather.13.mid = bf16[1536,256]{1,0:T(8,128)(2,1)S(1)} all-gather(bf16[192,256]{1,0:T(8,128)(2,1)S(1)} %add_convert_fusion), channel_id=1, replica_groups=mesh['y'=8,'x'=4,'z'=8,'c'=2] {'x','c'}, dimensions={0}, use_global_device_ids=true | all-gather | bytes 884736 | tf_op jit(solution)/shard_map/all_gather | solution.py:267
  51.9 0.0 copy-done.2
  51.9 0.0 copy-start.3
  51.9 0.8 %shard_map.195.solved = bf16[2,384,256]{2,1,0:T(8,128)(2,1)S(1)} custom-call(s32[1,128]{1,0:T(1,128)S(1)} %copy-done.5, bf16[1536,256]{1,0:T(8,128)(2,1)S(1)} %all_gather.13.mid, f32[2,384,256]{2,1,0:T(8,128)S(1)} %get-tuple-element.27.base, bf16[2,384,384]{2,1,0:T(8,128)(2,1)S(1)} %get-tuple-element.28.spread, bf16[2,384,384]{2,1,0:T(8,128)(2,1)S(1)} %copy-done.2), custom_call_target="tpu_custom_call" | custom-call | flops 301989888 | bytes 3342336 | tf_op jit(solution)/shard_map/pallas_call | solution.py:268
  52.7 1.9 %collective-permute-start.1 = (bf16[2,384,256]{2,1,0:T(8,128)(2,1)S(1)}, bf16[2,384,256]{2,1,0:T(8,128)(2,1)S(1)}, u32[]{:S(2)}, u32[]{:S(2)}) collective-permute-start(bf16[2,384,256]{2,1,0:T(8,128)(2,1)S(1)} %shard_map.195.solved), channel_id=1, source_target_pairs={{511,0},{1,2},{3,4},{5,6},{7,8},{9,10},{11,12},{13,14},{15,16},{17... | collective-permute-start | bytes 1179656 | tf_op jit(solution)/shard_map/ppermute | solution.py:280
  54.6 8.8 %collective-permute-start.2 = (bf16[2,384,256]{2,1,0:T(8,128)(2,1)S(1)}, bf16[2,384,256]{2,1,0:T(8,128)(2,1)S(1)}, u32[]{:S(2)}, u32[]{:S(2)}) collective-permute-start(bf16[2,384,256]{2,1,0:T(8,128)(2,1)S(1)} %shard_map.195.solved), channel_id=1, source_target_pairs={{510,0},{0,2},{2,4},{4,6},{6,8},{8,10},{10,12},{12,14},{14,16},{16... | collective-permute-start | bytes 1179656 | tf_op jit(solution)/shard_map/ppermute | solution.py:281
  63.5 0.0 copy-done.3
  63.5 1.6 %shard_map.196 = (f32[2,384,256]{2,1,0:T(8,128)S(1)}, bf16[24,256]{1,0:T(8,128)(2,1)}, bf16[4,24,256]{2,1,0:T(8,128)(2,1)}, bf16[2,384,256]{2,1,0:T(8,128)(2,1)}) custom-call(s32[1,128]{1,0:T(1,128)S(1)} %copy-done.5, s32[2,384]{1,0:T(2,128)S(1)} %copy-done.6, bf16[2,384,384]{2,1,0:T(8,128)(2,1)S(1)} %copy-done.1, bf16[2,384,256]{2,1,0:T(8,128)(2,1)S(1)} %copy-done.3, ...), custom_call_target="tpu_custom_call" | custom-call | flops 301989888 | bytes 3538944 | tf_op jit(solution)/shard_map/pallas_call | solution.py:283
  65.1 2.4 %all_gather.14.chip = bf16[4,384,256]{2,1,0:T(8,128)(2,1)S(1)} all-gather(bf16[2,384,256]{2,1,0:T(8,128)(2,1)S(1)} %shard_map.195.solved), channel_id=1, replica_groups=mesh['y'=8,'x'=4,'z'=8,'c'=2] {'c'}, dimensions={0}, use_global_device_ids=true | all-gather | bytes 1179648 | tf_op jit(solution)/shard_map/all_gather | solution.py:282
  67.5 0.0 collective-permute-done.1
  67.5 2.4 %all_gather.15.nearby = bf16[4,384,256]{2,1,0:T(8,128)(2,1)S(1)} all-gather(bf16[2,384,256]{2,1,0:T(8,128)(2,1)S(1)} %collective-permute-done.1), channel_id=1, replica_groups=mesh['y'=8,'x'=4,'z'=8,'c'=2] {'c'}, dimensions={0}, use_global_device_ids=true | all-gather | bytes 1179648 | tf_op jit(solution)/shard_map/all_gather | solution.py:293
  69.8 0.0 collective-permute-done.2.outer
  69.8 1.8 %shard_map.197 = bf16[2,384,256]{2,1,0:T(8,128)(2,1)} custom-call(s32[1,128]{1,0:T(1,128)S(1)} %copy-done.5, f32[2,384,256]{2,1,0:T(8,128)S(1)} %get-tuple-element.34.base, bf16[2,384,384]{2,1,0:T(8,128)(2,1)S(1)} %get-tuple-element.35.spread, bf16[2,384,384]{2,1,0:T(8,128)(2,1)S(1)} %copy-done, bf16[4,384,256]{2,1,0:T(8,128)(2,1)S(1)} %all_gather.14.chip, ...), custom_call_target="tpu_custom_call" | custom-call | flops 301989888 | bytes 4128768 | tf_op jit(solution)/shard_map/pallas_call | solution.py:294
  (1 shorter events, 0.0 us)
Async XLA Ops:
  0.6 29.3 %copy-start = (bf16[2,384,384]{2,1,0:T(8,128)(2,1)S(1)}, bf16[2,384,384]{2,1,0:T(8,128)(2,1)}, u32[]{:S(2)}) copy-start(bf16[2,384,384]{2,1,0:T(8,128)(2,1)} %inverse.3) | copy-start | bytes 1769476
  0.6 29.3 %copy-start.1 = (bf16[2,384,384]{2,1,0:T(8,128)(2,1)S(1)}, bf16[2,384,384]{2,1,0:T(8,128)(2,1)}, u32[]{:S(2)}) copy-start(bf16[2,384,384]{2,1,0:T(8,128)(2,1)} %panels.7) | copy-start | bytes 1769476
  2.4 27.5 %copy-start.4 = (s32[4,384]{1,0:T(4,128)S(1)}, s32[4,384]{1,0:T(4,128)}, u32[]{:S(2)}) copy-start(s32[4,384]{1,0:T(4,128)} %mid_rows.1) | copy-start | bytes 18436
  29.9 4.3 %copy-start.7 = (bf16[2,384,384]{2,1,0:T(8,128)(2,1)S(1)}, bf16[2,384,384]{2,1,0:T(8,128)(2,1)}, u32[]{:S(2)}) copy-start(bf16[2,384,384]{2,1,0:T(8,128)(2,1)} %panels.6) | copy-start | bytes 1769476
  29.9 4.3 %copy-start.8 = (bf16[2,384,256]{2,1,0:T(8,128)(2,1)S(1)}, bf16[2,384,256]{2,1,0:T(8,128)(2,1)}, u32[]{:S(2)}) copy-start(bf16[2,384,256]{2,1,0:T(8,128)(2,1)} %rhs.4) | copy-start | bytes 1179652
  29.9 4.3 %copy-start.9 = (s32[2,384]{1,0:T(2,128)S(1)}, s32[2,384]{1,0:T(2,128)}, u32[]{:S(2)}) copy-start(s32[2,384]{1,0:T(2,128)} %rows.2) | copy-start | bytes 9220
  31.0 3.3 %copy-start.6 = (s32[2,384]{1,0:T(2,128)S(1)}, s32[2,384]{1,0:T(2,128)}, u32[]{:S(2)}) copy-start(s32[2,384]{1,0:T(2,128)} %rows.3) | copy-start | bytes 9220
  31.0 6.7 %collective-permute-start = (bf16[192,256]{1,0:T(8,128)(2,1)S(1)}, bf16[192,256]{1,0:T(8,128)(2,1)S(1)}, u32[]{:S(2)}, u32[]{:S(2)}) collective-permute-start(bf16[192,256]{1,0:T(8,128)(2,1)S(1)} %get-tuple-element.24), channel_id=1, source_target_pairs={{0,64},{64,0},{128,192},{192,128},{256,320},{320,256},{384,448},{4... | collective-permute-start | bytes 294920 | tf_op jit(solution)/shard_map/ppermute | solution.py:257
  34.2 0.7 copy-start.5
  37.7 14.2 %copy-start.2 = (bf16[2,384,384]{2,1,0:T(8,128)(2,1)S(1)}, bf16[2,384,384]{2,1,0:T(8,128)(2,1)}, u32[]{:S(2)}) copy-start(bf16[2,384,384]{2,1,0:T(8,128)(2,1)} %inverse.2) | copy-start | bytes 1769476
  51.9 11.6 %copy-start.3 = (bf16[2,384,256]{2,1,0:T(8,128)(2,1)S(1)}, bf16[2,384,256]{2,1,0:T(8,128)(2,1)}, u32[]{:S(2)}) copy-start(bf16[2,384,256]{2,1,0:T(8,128)(2,1)} %rhs.5) | copy-start | bytes 1179652
  52.7 14.8 %collective-permute-start.1 = (bf16[2,384,256]{2,1,0:T(8,128)(2,1)S(1)}, bf16[2,384,256]{2,1,0:T(8,128)(2,1)S(1)}, u32[]{:S(2)}, u32[]{:S(2)}) collective-permute-start(bf16[2,384,256]{2,1,0:T(8,128)(2,1)S(1)} %shard_map.195.solved), channel_id=1, source_target_pairs={{511,0},{1,2},{3,4},{5,6},{7,8},{9,10},{11,12},{13,14},{15,16},{17... | collective-permute-start | bytes 1179656 | tf_op jit(solution)/shard_map/ppermute | solution.py:280
  54.6 15.2 %collective-permute-start.2 = (bf16[2,384,256]{2,1,0:T(8,128)(2,1)S(1)}, bf16[2,384,256]{2,1,0:T(8,128)(2,1)S(1)}, u32[]{:S(2)}, u32[]{:S(2)}) collective-permute-start(bf16[2,384,256]{2,1,0:T(8,128)(2,1)S(1)} %shard_map.195.solved), channel_id=1, source_target_pairs={{510,0},{0,2},{2,4},{4,6},{6,8},{8,10},{10,12},{12,14},{14,16},{16... | collective-permute-start | bytes 1179656 | tf_op jit(solution)/shard_map/ppermute | solution.py:281

commit v6 on v5

--- a/solution.py
+++ b/solution.py
@@ -114,8 +114,8 @@
     mid_index = mid_rows[pl.ds(lax.axis_index("x"), 1), :]
     solved = dot(got[:, :W], got[:, W : W + K]).astype(BF16)
     root[...] = solved
-    picked = dot(one_hot(mid_index, 0, W // LANE), solved).astype(BF16)
-    products = dot(got[:, W + 2 * K + LANE :].T, picked)
+    spread = dot(got[:, W + 2 * K + LANE :].T, one_hot(mid_index, 0, W // LANE)).astype(BF16)
+    products = dot(spread, solved)
     first = pl.multiple_of(side * HALF, 64)
     rhs = got[pl.ds(first, HALF), W + K : W + 2 * K].astype(F32)
     update = (rhs - products[:HALF]).astype(BF16)

time: 72 us -> 71.7 us (level)
  no operation moved by 1% of the time
where the time goes in v6:
time: 71.7 us; the launch traced here: 71.3 us
  blocking collectives  46.4 us (65%)
  starting transfers between devices  14 us (20%)
  Pallas kernels  9.45 us (13%)
  between operations  0.83 us (1%)
    all_gather x1, blocking collectives, per_device(): got = lax.all_gather(packed, ROWS, axis=0, tiled=True)  27.5 us
    all_gather x1, blocking collectives, per_device(): mid = lax.all_gather(mid_half, ('x', 'c'), axis=0, tiled=True)  14.1 us
    ppermute x1, starting transfers between devices, per_device(): outer = lax.ppermute(solved, ALL, straight)  8.84 us
    ppermute x1, starting transfers between devices, per_device(): lax.ppermute(part, 'y', [(i, i ^ 1) for i in range(lax.axis_size('y'))])  3.21 us
    pallas_call x1, Pallas kernels, per_device(): call(ready_kernel, (tall, square, tall, square), [VMEM] * 7, 16 * W * W *...  2.77 us
    all_gather x1, blocking collectives, per_device(): chip = lax.all_gather(solved, 'c', axis=0, tiled=True)  2.37 us
    all_gather x1, blocking collectives, per_device(): nearby = lax.all_gather(inner, 'c', axis=0, tiled=True)  2.36 us
    ppermute x1, starting transfers between devices, per_device(): inner = lax.ppermute(solved, ALL, cross)  1.92 us
  transfers between devices with their start and end apart: 3, of which 0 were waited for; matrix products, arithmetic and copies ran while one was open for 0% of the time, Pallas kernels for 6%

profile of v6, /device:TPU:1, one launch (start us, length us, event | category | flops | bytes accessed | tf_op | source)
XLA Modules:
  0.0 71.3 jit_solution(8262587889844522977)
XLA Ops:
  0.6 0.0 copy-start
  0.6 0.0 copy-start.1
  0.7 1.7 %shard_map.192 = (bf16[24,1280]{1,0:T(8,128)(2,1)}, s32[1,128]{1,0:T(1,128)}) custom-call(bf16[24,384]{1,0:T(8,128)(2,1)} %root_inverse.1, bf16[24,256]{1,0:T(8,128)(2,1)} %root_rhs.1, bf16[4,24,384]{2,1,0:T(8,128)(2,1)} %panels.4, bf16[4,24,384]{2,1,0:T(8,128)(2,1)} %inverses.2, bf16[4,24,256]{2,1,0:T(8,128)(2,1)} %rhs.3, s32[1024]{0:T(1024)} %bitcast.1, ...), custom_call_target="tpu_custom_call" | custom-call | bytes 122880 | tf_op jit(solution)/shard_map/pallas_call | solution.py:236
  2.4 0.0 copy-start.4
  2.4 27.5 %all_gather.12.got = bf16[384,1280]{1,0:T(8,128)(2,1)S(1)} all-gather(bf16[24,1280]{1,0:T(8,128)(2,1)} %get-tuple-element.22), channel_id=1, replica_groups=mesh['y'=8,'x'=4,'z'=8,'c'=2] {'z','c'}, dimensions={0}, use_global_device_ids=true | all-gather | bytes 1044480 | tf_op jit(solution)/shard_map/all_gather | solution.py:247
  29.9 0.0 copy-done
  29.9 0.0 copy-done.1
  29.9 0.0 copy-done.4
  29.9 0.0 copy-start.7
  29.9 0.0 copy-start.8
  29.9 0.0 copy-start.9
  30.0 0.8 %shard_map.193 = (bf16[384,256]{1,0:T(8,128)(2,1)S(1)}, bf16[192,256]{1,0:T(8,128)(2,1)S(1)}) custom-call(bf16[384,1280]{1,0:T(8,128)(2,1)S(1)} %all_gather.12.got, s32[4,384]{1,0:T(4,128)S(1)} %copy-done.4, bf16[2,384,384]{2,1,0:T(8,128)(2,1)S(1)} %copy-done.1, bf16[2,384,384]{2,1,0:T(8,128)(2,1)S(1)} %copy-done), custom_call_target="tpu_custom_call" | custom-call | flops 150994944 | bytes 983040 | tf_op jit(solution)/shard_map/pallas_call | solution.py:250
  30.8 0.0 copy-start.6
  30.8 3.2 %collective-permute-start = (bf16[192,256]{1,0:T(8,128)(2,1)S(1)}, bf16[192,256]{1,0:T(8,128)(2,1)S(1)}, u32[]{:S(2)}, u32[]{:S(2)}) collective-permute-start(bf16[192,256]{1,0:T(8,128)(2,1)S(1)} %get-tuple-element.24), channel_id=1, source_target_pairs={{0,64},{64,0},{128,192},{192,128},{256,320},{320,256},{384,448},{4... | collective-permute-start | bytes 294920 | tf_op jit(solution)/shard_map/ppermute | solution.py:257
  34.0 0.0 copy-start.5
  34.0 0.0 copy-done.7
  34.0 0.0 copy-done.8
  34.0 0.0 copy-done.9
  34.0 0.0 copy-done.6
  34.0 0.6 copy-done.5
  34.6 2.8 %shard_map.194 = (f32[2,384,256]{2,1,0:T(8,128)S(1)}, bf16[2,384,384]{2,1,0:T(8,128)(2,1)S(1)}, f32[2,384,256]{2,1,0:T(8,128)S(1)}, bf16[2,384,384]{2,1,0:T(8,128)(2,1)S(1)}) custom-call(s32[2,384]{1,0:T(2,128)S(1)} %copy-done.9, bf16[2,384,384]{2,1,0:T(8,128)(2,1)S(1)} %copy-done.7, bf16[2,384,256]{2,1,0:T(8,128)(2,1)S(1)} %copy-done.8, ...), custom_call_target="tpu_custom_call" | custom-call | flops 1207959552 | bytes 6291456 | tf_op jit(solution)/shard_map/pallas_call | solution.py:258
  37.4 0.0 copy-start.2
  37.4 0.0 collective-permute-done
  37.5 14.1 %all_gather.13.mid = bf16[1536,256]{1,0:T(8,128)(2,1)S(1)} all-gather(bf16[192,256]{1,0:T(8,128)(2,1)S(1)} %add_convert_fusion), channel_id=1, replica_groups=mesh['y'=8,'x'=4,'z'=8,'c'=2] {'x','c'}, dimensions={0}, use_global_device_ids=true | all-gather | bytes 884736 | tf_op jit(solution)/shard_map/all_gather | solution.py:267
  51.6 0.0 copy-done.2
  51.6 0.0 copy-start.3
  51.6 0.8 %shard_map.195.solved = bf16[2,384,256]{2,1,0:T(8,128)(2,1)S(1)} custom-call(s32[1,128]{1,0:T(1,128)S(1)} %copy-done.5, bf16[1536,256]{1,0:T(8,128)(2,1)S(1)} %all_gather.13.mid, f32[2,384,256]{2,1,0:T(8,128)S(1)} %get-tuple-element.27.base, bf16[2,384,384]{2,1,0:T(8,128)(2,1)S(1)} %get-tuple-element.28.spread, bf16[2,384,384]{2,1,0:T(8,128)(2,1)S(1)} %copy-done.2), custom_call_target="tpu_custom_call" | custom-call | flops 301989888 | bytes 3342336 | tf_op jit(solution)/shard_map/pallas_call | solution.py:268
  52.4 1.9 %collective-permute-start.1 = (bf16[2,384,256]{2,1,0:T(8,128)(2,1)S(1)}, bf16[2,384,256]{2,1,0:T(8,128)(2,1)S(1)}, u32[]{:S(2)}, u32[]{:S(2)}) collective-permute-start(bf16[2,384,256]{2,1,0:T(8,128)(2,1)S(1)} %shard_map.195.solved), channel_id=1, source_target_pairs={{511,0},{1,2},{3,4},{5,6},{7,8},{9,10},{11,12},{13,14},{15,16},{17... | collective-permute-start | bytes 1179656 | tf_op jit(solution)/shard_map/ppermute | solution.py:280
  54.4 8.8 %collective-permute-start.2 = (bf16[2,384,256]{2,1,0:T(8,128)(2,1)S(1)}, bf16[2,384,256]{2,1,0:T(8,128)(2,1)S(1)}, u32[]{:S(2)}, u32[]{:S(2)}) collective-permute-start(bf16[2,384,256]{2,1,0:T(8,128)(2,1)S(1)} %shard_map.195.solved), channel_id=1, source_target_pairs={{510,0},{0,2},{2,4},{4,6},{6,8},{8,10},{10,12},{12,14},{14,16},{16... | collective-permute-start | bytes 1179656 | tf_op jit(solution)/shard_map/ppermute | solution.py:281
  63.2 0.0 copy-done.3
  63.2 1.6 %shard_map.196 = (f32[2,384,256]{2,1,0:T(8,128)S(1)}, bf16[24,256]{1,0:T(8,128)(2,1)}, bf16[4,24,256]{2,1,0:T(8,128)(2,1)}, bf16[2,384,256]{2,1,0:T(8,128)(2,1)}) custom-call(s32[1,128]{1,0:T(1,128)S(1)} %copy-done.5, s32[2,384]{1,0:T(2,128)S(1)} %copy-done.6, bf16[2,384,384]{2,1,0:T(8,128)(2,1)S(1)} %copy-done.1, bf16[2,384,256]{2,1,0:T(8,128)(2,1)S(1)} %copy-done.3, ...), custom_call_target="tpu_custom_call" | custom-call | flops 301989888 | bytes 3538944 | tf_op jit(solution)/shard_map/pallas_call | solution.py:283
  64.8 2.4 %all_gather.14.chip = bf16[4,384,256]{2,1,0:T(8,128)(2,1)S(1)} all-gather(bf16[2,384,256]{2,1,0:T(8,128)(2,1)S(1)} %shard_map.195.solved), channel_id=1, replica_groups=mesh['y'=8,'x'=4,'z'=8,'c'=2] {'c'}, dimensions={0}, use_global_device_ids=true | all-gather | bytes 1179648 | tf_op jit(solution)/shard_map/all_gather | solution.py:282
  67.2 0.0 collective-permute-done.1
  67.2 2.4 %all_gather.15.nearby = bf16[4,384,256]{2,1,0:T(8,128)(2,1)S(1)} all-gather(bf16[2,384,256]{2,1,0:T(8,128)(2,1)S(1)} %collective-permute-done.1), channel_id=1, replica_groups=mesh['y'=8,'x'=4,'z'=8,'c'=2] {'c'}, dimensions={0}, use_global_device_ids=true | all-gather | bytes 1179648 | tf_op jit(solution)/shard_map/all_gather | solution.py:293
  69.6 0.0 collective-permute-done.2.outer
  69.6 1.8 %shard_map.197 = bf16[2,384,256]{2,1,0:T(8,128)(2,1)} custom-call(s32[1,128]{1,0:T(1,128)S(1)} %copy-done.5, f32[2,384,256]{2,1,0:T(8,128)S(1)} %get-tuple-element.34.base, bf16[2,384,384]{2,1,0:T(8,128)(2,1)S(1)} %get-tuple-element.35.spread, bf16[2,384,384]{2,1,0:T(8,128)(2,1)S(1)} %copy-done, bf16[4,384,256]{2,1,0:T(8,128)(2,1)S(1)} %all_gather.14.chip, ...), custom_call_target="tpu_custom_call" | custom-call | flops 301989888 | bytes 4128768 | tf_op jit(solution)/shard_map/pallas_call | solution.py:294
  (1 shorter events, 0.0 us)
Async XLA Ops:
  0.6 29.3 %copy-start = (bf16[2,384,384]{2,1,0:T(8,128)(2,1)S(1)}, bf16[2,384,384]{2,1,0:T(8,128)(2,1)}, u32[]{:S(2)}) copy-start(bf16[2,384,384]{2,1,0:T(8,128)(2,1)} %inverse.3) | copy-start | bytes 1769476
  0.6 29.3 %copy-start.1 = (bf16[2,384,384]{2,1,0:T(8,128)(2,1)S(1)}, bf16[2,384,384]{2,1,0:T(8,128)(2,1)}, u32[]{:S(2)}) copy-start(bf16[2,384,384]{2,1,0:T(8,128)(2,1)} %panels.7) | copy-start | bytes 1769476
  2.4 27.5 %copy-start.4 = (s32[4,384]{1,0:T(4,128)S(1)}, s32[4,384]{1,0:T(4,128)}, u32[]{:S(2)}) copy-start(s32[4,384]{1,0:T(4,128)} %mid_rows.1) | copy-start | bytes 18436
  29.9 4.1 %copy-start.7 = (bf16[2,384,384]{2,1,0:T(8,128)(2,1)S(1)}, bf16[2,384,384]{2,1,0:T(8,128)(2,1)}, u32[]{:S(2)}) copy-start(bf16[2,384,384]{2,1,0:T(8,128)(2,1)} %panels.6) | copy-start | bytes 1769476
  29.9 4.1 %copy-start.8 = (bf16[2,384,256]{2,1,0:T(8,128)(2,1)S(1)}, bf16[2,384,256]{2,1,0:T(8,128)(2,1)}, u32[]{:S(2)}) copy-start(bf16[2,384,256]{2,1,0:T(8,128)(2,1)} %rhs.4) | copy-start | bytes 1179652
  29.9 4.1 %copy-start.9 = (s32[2,384]{1,0:T(2,128)S(1)}, s32[2,384]{1,0:T(2,128)}, u32[]{:S(2)}) copy-start(s32[2,384]{1,0:T(2,128)} %rows.2) | copy-start | bytes 9220
  30.8 3.3 %copy-start.6 = (s32[2,384]{1,0:T(2,128)S(1)}, s32[2,384]{1,0:T(2,128)}, u32[]{:S(2)}) copy-start(s32[2,384]{1,0:T(2,128)} %rows.3) | copy-start | bytes 9220
  30.8 6.7 %collective-permute-start = (bf16[192,256]{1,0:T(8,128)(2,1)S(1)}, bf16[192,256]{1,0:T(8,128)(2,1)S(1)}, u32[]{:S(2)}, u32[]{:S(2)}) collective-permute-start(bf16[192,256]{1,0:T(8,128)(2,1)S(1)} %get-tuple-element.24), channel_id=1, source_target_pairs={{0,64},{64,0},{128,192},{192,128},{256,320},{320,256},{384,448},{4... | collective-permute-start | bytes 294920 | tf_op jit(solution)/shard_map/ppermute | solution.py:257
  34.0 0.7 copy-start.5
  37.4 14.2 %copy-start.2 = (bf16[2,384,384]{2,1,0:T(8,128)(2,1)S(1)}, bf16[2,384,384]{2,1,0:T(8,128)(2,1)}, u32[]{:S(2)}) copy-start(bf16[2,384,384]{2,1,0:T(8,128)(2,1)} %inverse.2) | copy-start | bytes 1769476
  51.6 11.6 %copy-start.3 = (bf16[2,384,256]{2,1,0:T(8,128)(2,1)S(1)}, bf16[2,384,256]{2,1,0:T(8,128)(2,1)}, u32[]{:S(2)}) copy-start(bf16[2,384,256]{2,1,0:T(8,128)(2,1)} %rhs.5) | copy-start | bytes 1179652
  52.4 14.8 %collective-permute-start.1 = (bf16[2,384,256]{2,1,0:T(8,128)(2,1)S(1)}, bf16[2,384,256]{2,1,0:T(8,128)(2,1)S(1)}, u32[]{:S(2)}, u32[]{:S(2)}) collective-permute-start(bf16[2,384,256]{2,1,0:T(8,128)(2,1)S(1)} %shard_map.195.solved), channel_id=1, source_target_pairs={{511,0},{1,2},{3,4},{5,6},{7,8},{9,10},{11,12},{13,14},{15,16},{17... | collective-permute-start | bytes 1179656 | tf_op jit(solution)/shard_map/ppermute | solution.py:280
  54.4 15.2 %collective-permute-start.2 = (bf16[2,384,256]{2,1,0:T(8,128)(2,1)S(1)}, bf16[2,384,256]{2,1,0:T(8,128)(2,1)S(1)}, u32[]{:S(2)}, u32[]{:S(2)}) collective-permute-start(bf16[2,384,256]{2,1,0:T(8,128)(2,1)S(1)} %shard_map.195.solved), channel_id=1, source_target_pairs={{510,0},{0,2},{2,4},{4,6},{6,8},{8,10},{10,12},{12,14},{14,16},{16... | collective-permute-start | bytes 1179656 | tf_op jit(solution)/shard_map/ppermute | solution.py:281

commit v7 on v6

--- a/solution.py
+++ b/solution.py
@@ -175,17 +175,19 @@
     root_own[...] = dot(own, root[...]).astype(BF16)
     for s in range(mid_own.shape[0]):
         mid_own[s] = dot(own, mid[s * W : (s + 1) * W, :]).astype(BF16)
-    for n in range(2):
-        index = rows[n : n + 1, :]
-        above = rows_of(mid, fact(facts, 5 * n + 1))
-        picked = dot(one_hot(index, W, W // LANE), above).astype(BF16)
-        base[n] = rhs[n].astype(F32) - from_root[n] - dot(panels[n].T, picked)
+    picked = [
+        dot(one_hot(rows[n : n + 1, :], W, W // LANE), rows_of(mid, fact(facts, 5 * n + 1))).astype(BF16)
+        for n in range(2)
+    ]
+    for n in range(2):
+        base[n] = rhs[n].astype(F32) - from_root[n] - dot(panels[n].T, picked[n])
     store.wait()
 
 
 def leaf_kernel(facts, base, spread, inverse, chip, nearby, outer, out, held, done, sems):
-    for n in range(2):
-        block, member = fact(facts, 5 * n + 2), fact(facts, 5 * n + 3)
+    numbers = [[fact(facts, 5 * n + i) for i in (2, 3, 4)] for n in range(2)]
+    for n in range(2):
+        block, member, _ = numbers[n]
 
         @pl.when(jnp.logical_or(block == 0, block == 1))
         def _():
@@ -204,7 +206,7 @@
     stores = []
     for n in range(2):
         solved = dot(inverse[n], updates[n])
-        done[n] = jnp.where(row < fact(facts, 5 * n + 4), solved, 0.0).astype(BF16)
+        done[n] = jnp.where(row < numbers[n][2], solved, 0.0).astype(BF16)
         stores.append(pltpu.make_async_copy(done.at[n], out.at[n], sems.at[n]))
         stores[n].start()
     for store in stores:

time: 71.7 us -> 71.6 us (level)
  no operation moved by 1% of the time
where the time goes in v7:
time: 71.6 us; the launch traced here: 71.2 us
  blocking collectives  46.4 us (65%)
  starting transfers between devices  14 us (20%)
  Pallas kernels  9.3 us (13%)
  between operations  0.83 us (1%)
    all_gather x1, blocking collectives, per_device(): got = lax.all_gather(packed, ROWS, axis=0, tiled=True)  27.5 us
    all_gather x1, blocking collectives, per_device(): mid = lax.all_gather(mid_half, ('x', 'c'), axis=0, tiled=True)  14.1 us
    ppermute x1, starting transfers between devices, per_device(): outer = lax.ppermute(solved, ALL, straight)  8.84 us
    ppermute x1, starting transfers between devices, per_device(): lax.ppermute(part, 'y', [(i, i ^ 1) for i in range(lax.axis_size('y'))])  3.21 us
    pallas_call x1, Pallas kernels, per_device(): call(ready_kernel, (tall, square, tall, square), [VMEM] * 7, 16 * W * W *...  2.77 us
    all_gather x1, blocking collectives, per_device(): chip = lax.all_gather(solved, 'c', axis=0, tiled=True)  2.37 us
    all_gather x1, blocking collectives, per_device(): nearby = lax.all_gather(inner, 'c', axis=0, tiled=True)  2.36 us
    ppermute x1, starting transfers between devices, per_device(): inner = lax.ppermute(solved, ALL, cross)  1.92 us
  transfers between devices with their start and end apart: 3, of which 0 were waited for; matrix products, arithmetic and copies ran while one was open for 0% of the time, Pallas kernels for 6%

profile of v7, /device:TPU:1, one launch (start us, length us, event | category | flops | bytes accessed | tf_op | source)
XLA Modules:
  0.0 71.2 jit_solution(10931646004662354431)
XLA Ops:
  0.6 0.0 copy-start
  0.6 0.0 copy-start.1
  0.7 1.7 %shard_map.192 = (bf16[24,1280]{1,0:T(8,128)(2,1)}, s32[1,128]{1,0:T(1,128)}) custom-call(bf16[24,384]{1,0:T(8,128)(2,1)} %root_inverse.1, bf16[24,256]{1,0:T(8,128)(2,1)} %root_rhs.1, bf16[4,24,384]{2,1,0:T(8,128)(2,1)} %panels.4, bf16[4,24,384]{2,1,0:T(8,128)(2,1)} %inverses.2, bf16[4,24,256]{2,1,0:T(8,128)(2,1)} %rhs.3, s32[1024]{0:T(1024)} %bitcast.1, ...), custom_call_target="tpu_custom_call" | custom-call | bytes 122880 | tf_op jit(solution)/shard_map/pallas_call | solution.py:238
  2.4 0.0 copy-start.4
  2.4 27.5 %all_gather.12.got = bf16[384,1280]{1,0:T(8,128)(2,1)S(1)} all-gather(bf16[24,1280]{1,0:T(8,128)(2,1)} %get-tuple-element.22), channel_id=1, replica_groups=mesh['y'=8,'x'=4,'z'=8,'c'=2] {'z','c'}, dimensions={0}, use_global_device_ids=true | all-gather | bytes 1044480 | tf_op jit(solution)/shard_map/all_gather | solution.py:249
  29.9 0.0 copy-done
  29.9 0.0 copy-done.1
  29.9 0.0 copy-done.4
  29.9 0.0 copy-start.7
  29.9 0.0 copy-start.8
  29.9 0.0 copy-start.9
  30.0 0.8 %shard_map.193 = (bf16[384,256]{1,0:T(8,128)(2,1)S(1)}, bf16[192,256]{1,0:T(8,128)(2,1)S(1)}) custom-call(bf16[384,1280]{1,0:T(8,128)(2,1)S(1)} %all_gather.12.got, s32[4,384]{1,0:T(4,128)S(1)} %copy-done.4, bf16[2,384,384]{2,1,0:T(8,128)(2,1)S(1)} %copy-done.1, bf16[2,384,384]{2,1,0:T(8,128)(2,1)S(1)} %copy-done), custom_call_target="tpu_custom_call" | custom-call | flops 150994944 | bytes 983040 | tf_op jit(solution)/shard_map/pallas_call | solution.py:252
  30.8 0.0 copy-start.6
  30.8 3.2 %collective-permute-start = (bf16[192,256]{1,0:T(8,128)(2,1)S(1)}, bf16[192,256]{1,0:T(8,128)(2,1)S(1)}, u32[]{:S(2)}, u32[]{:S(2)}) collective-permute-start(bf16[192,256]{1,0:T(8,128)(2,1)S(1)} %get-tuple-element.24), channel_id=1, source_target_pairs={{0,64},{64,0},{128,192},{192,128},{256,320},{320,256},{384,448},{4... | collective-permute-start | bytes 294920 | tf_op jit(solution)/shard_map/ppermute | solution.py:259
  34.0 0.0 copy-start.5
  34.0 0.0 copy-done.7
  34.0 0.0 copy-done.8
  34.0 0.0 copy-done.9
  34.0 0.0 copy-done.6
  34.0 0.6 copy-done.5
  34.6 2.8 %shard_map.194 = (f32[2,384,256]{2,1,0:T(8,128)S(1)}, bf16[2,384,384]{2,1,0:T(8,128)(2,1)S(1)}, f32[2,384,256]{2,1,0:T(8,128)S(1)}, bf16[2,384,384]{2,1,0:T(8,128)(2,1)S(1)}) custom-call(s32[2,384]{1,0:T(2,128)S(1)} %copy-done.9, bf16[2,384,384]{2,1,0:T(8,128)(2,1)S(1)} %copy-done.7, bf16[2,384,256]{2,1,0:T(8,128)(2,1)S(1)} %copy-done.8, ...), custom_call_target="tpu_custom_call" | custom-call | flops 1207959552 | bytes 6291456 | tf_op jit(solution)/shard_map/pallas_call | solution.py:260
  37.4 0.0 copy-start.2
  37.4 0.0 collective-permute-done
  37.5 14.1 %all_gather.13.mid = bf16[1536,256]{1,0:T(8,128)(2,1)S(1)} all-gather(bf16[192,256]{1,0:T(8,128)(2,1)S(1)} %add_convert_fusion), channel_id=1, replica_groups=mesh['y'=8,'x'=4,'z'=8,'c'=2] {'x','c'}, dimensions={0}, use_global_device_ids=true | all-gather | bytes 884736 | tf_op jit(solution)/shard_map/all_gather | solution.py:269
  51.6 0.0 copy-done.2
  51.6 0.0 copy-start.3
  51.6 0.8 %shard_map.195.solved = bf16[2,384,256]{2,1,0:T(8,128)(2,1)S(1)} custom-call(s32[1,128]{1,0:T(1,128)S(1)} %copy-done.5, bf16[1536,256]{1,0:T(8,128)(2,1)S(1)} %all_gather.13.mid, f32[2,384,256]{2,1,0:T(8,128)S(1)} %get-tuple-element.27.base, bf16[2,384,384]{2,1,0:T(8,128)(2,1)S(1)} %get-tuple-element.28.spread, bf16[2,384,384]{2,1,0:T(8,128)(2,1)S(1)} %copy-done.2), custom_call_target="tpu_custom_call" | custom-call | flops 301989888 | bytes 3342336 | tf_op jit(solution)/shard_map/pallas_call | solution.py:270
  52.4 1.9 %collective-permute-start.1 = (bf16[2,384,256]{2,1,0:T(8,128)(2,1)S(1)}, bf16[2,384,256]{2,1,0:T(8,128)(2,1)S(1)}, u32[]{:S(2)}, u32[]{:S(2)}) collective-permute-start(bf16[2,384,256]{2,1,0:T(8,128)(2,1)S(1)} %shard_map.195.solved), channel_id=1, source_target_pairs={{511,0},{1,2},{3,4},{5,6},{7,8},{9,10},{11,12},{13,14},{15,16},{17... | collective-permute-start | bytes 1179656 | tf_op jit(solution)/shard_map/ppermute | solution.py:282
  54.4 8.8 %collective-permute-start.2 = (bf16[2,384,256]{2,1,0:T(8,128)(2,1)S(1)}, bf16[2,384,256]{2,1,0:T(8,128)(2,1)S(1)}, u32[]{:S(2)}, u32[]{:S(2)}) collective-permute-start(bf16[2,384,256]{2,1,0:T(8,128)(2,1)S(1)} %shard_map.195.solved), channel_id=1, source_target_pairs={{510,0},{0,2},{2,4},{4,6},{6,8},{8,10},{10,12},{12,14},{14,16},{16... | collective-permute-start | bytes 1179656 | tf_op jit(solution)/shard_map/ppermute | solution.py:283
  63.2 0.0 copy-done.3
  63.2 1.6 %shard_map.196 = (f32[2,384,256]{2,1,0:T(8,128)S(1)}, bf16[24,256]{1,0:T(8,128)(2,1)}, bf16[4,24,256]{2,1,0:T(8,128)(2,1)}, bf16[2,384,256]{2,1,0:T(8,128)(2,1)}) custom-call(s32[1,128]{1,0:T(1,128)S(1)} %copy-done.5, s32[2,384]{1,0:T(2,128)S(1)} %copy-done.6, bf16[2,384,384]{2,1,0:T(8,128)(2,1)S(1)} %copy-done.1, bf16[2,384,256]{2,1,0:T(8,128)(2,1)S(1)} %copy-done.3, ...), custom_call_target="tpu_custom_call" | custom-call | flops 301989888 | bytes 3538944 | tf_op jit(solution)/shard_map/pallas_call | solution.py:285
  64.8 2.4 %all_gather.14.chip = bf16[4,384,256]{2,1,0:T(8,128)(2,1)S(1)} all-gather(bf16[2,384,256]{2,1,0:T(8,128)(2,1)S(1)} %shard_map.195.solved), channel_id=1, replica_groups=mesh['y'=8,'x'=4,'z'=8,'c'=2] {'c'}, dimensions={0}, use_global_device_ids=true | all-gather | bytes 1179648 | tf_op jit(solution)/shard_map/all_gather | solution.py:284
  67.2 0.0 collective-permute-done.1
  67.2 2.4 %all_gather.15.nearby = bf16[4,384,256]{2,1,0:T(8,128)(2,1)S(1)} all-gather(bf16[2,384,256]{2,1,0:T(8,128)(2,1)S(1)} %collective-permute-done.1), channel_id=1, replica_groups=mesh['y'=8,'x'=4,'z'=8,'c'=2] {'c'}, dimensions={0}, use_global_device_ids=true | all-gather | bytes 1179648 | tf_op jit(solution)/shard_map/all_gather | solution.py:295
  69.5 0.0 collective-permute-done.2.outer
  69.5 1.6 %shard_map.197 = bf16[2,384,256]{2,1,0:T(8,128)(2,1)} custom-call(s32[1,128]{1,0:T(1,128)S(1)} %copy-done.5, f32[2,384,256]{2,1,0:T(8,128)S(1)} %get-tuple-element.34.base, bf16[2,384,384]{2,1,0:T(8,128)(2,1)S(1)} %get-tuple-element.35.spread, bf16[2,384,384]{2,1,0:T(8,128)(2,1)S(1)} %copy-done, bf16[4,384,256]{2,1,0:T(8,128)(2,1)S(1)} %all_gather.14.chip, ...), custom_call_target="tpu_custom_call" | custom-call | flops 301989888 | bytes 4128768 | tf_op jit(solution)/shard_map/pallas_call | solution.py:296
  (1 shorter events, 0.0 us)
Async XLA Ops:
  0.6 29.3 %copy-start = (bf16[2,384,384]{2,1,0:T(8,128)(2,1)S(1)}, bf16[2,384,384]{2,1,0:T(8,128)(2,1)}, u32[]{:S(2)}) copy-start(bf16[2,384,384]{2,1,0:T(8,128)(2,1)} %inverse.3) | copy-start | bytes 1769476
  0.6 29.3 %copy-start.1 = (bf16[2,384,384]{2,1,0:T(8,128)(2,1)S(1)}, bf16[2,384,384]{2,1,0:T(8,128)(2,1)}, u32[]{:S(2)}) copy-start(bf16[2,384,384]{2,1,0:T(8,128)(2,1)} %panels.7) | copy-start | bytes 1769476
  2.4 27.5 %copy-start.4 = (s32[4,384]{1,0:T(4,128)S(1)}, s32[4,384]{1,0:T(4,128)}, u32[]{:S(2)}) copy-start(s32[4,384]{1,0:T(4,128)} %mid_rows.1) | copy-start | bytes 18436
  29.9 4.1 %copy-start.7 = (bf16[2,384,384]{2,1,0:T(8,128)(2,1)S(1)}, bf16[2,384,384]{2,1,0:T(8,128)(2,1)}, u32[]{:S(2)}) copy-start(bf16[2,384,384]{2,1,0:T(8,128)(2,1)} %panels.6) | copy-start | bytes 1769476
  29.9 4.1 %copy-start.8 = (bf16[2,384,256]{2,1,0:T(8,128)(2,1)S(1)}, bf16[2,384,256]{2,1,0:T(8,128)(2,1)}, u32[]{:S(2)}) copy-start(bf16[2,384,256]{2,1,0:T(8,128)(2,1)} %rhs.4) | copy-start | bytes 1179652
  29.9 4.1 %copy-start.9 = (s32[2,384]{1,0:T(2,128)S(1)}, s32[2,384]{1,0:T(2,128)}, u32[]{:S(2)}) copy-start(s32[2,384]{1,0:T(2,128)} %rows.2) | copy-start | bytes 9220
  30.8 3.3 %copy-start.6 = (s32[2,384]{1,0:T(2,128)S(1)}, s32[2,384]{1,0:T(2,128)}, u32[]{:S(2)}) copy-start(s32[2,384]{1,0:T(2,128)} %rows.3) | copy-start | bytes 9220
  30.8 6.7 %collective-permute-start = (bf16[192,256]{1,0:T(8,128)(2,1)S(1)}, bf16[192,256]{1,0:T(8,128)(2,1)S(1)}, u32[]{:S(2)}, u32[]{:S(2)}) collective-permute-start(bf16[192,256]{1,0:T(8,128)(2,1)S(1)} %get-tuple-element.24), channel_id=1, source_target_pairs={{0,64},{64,0},{128,192},{192,128},{256,320},{320,256},{384,448},{4... | collective-permute-start | bytes 294920 | tf_op jit(solution)/shard_map/ppermute | solution.py:259
  34.0 0.7 copy-start.5
  37.4 14.2 %copy-start.2 = (bf16[2,384,384]{2,1,0:T(8,128)(2,1)S(1)}, bf16[2,384,384]{2,1,0:T(8,128)(2,1)}, u32[]{:S(2)}) copy-start(bf16[2,384,384]{2,1,0:T(8,128)(2,1)} %inverse.2) | copy-start | bytes 1769476
  51.6 11.6 %copy-start.3 = (bf16[2,384,256]{2,1,0:T(8,128)(2,1)S(1)}, bf16[2,384,256]{2,1,0:T(8,128)(2,1)}, u32[]{:S(2)}) copy-start(bf16[2,384,256]{2,1,0:T(8,128)(2,1)} %rhs.5) | copy-start | bytes 1179652
  52.4 14.8 %collective-permute-start.1 = (bf16[2,384,256]{2,1,0:T(8,128)(2,1)S(1)}, bf16[2,384,256]{2,1,0:T(8,128)(2,1)S(1)}, u32[]{:S(2)}, u32[]{:S(2)}) collective-permute-start(bf16[2,384,256]{2,1,0:T(8,128)(2,1)S(1)} %shard_map.195.solved), channel_id=1, source_target_pairs={{511,0},{1,2},{3,4},{5,6},{7,8},{9,10},{11,12},{13,14},{15,16},{17... | collective-permute-start | bytes 1179656 | tf_op jit(solution)/shard_map/ppermute | solution.py:282
  54.4 15.2 %collective-permute-start.2 = (bf16[2,384,256]{2,1,0:T(8,128)(2,1)S(1)}, bf16[2,384,256]{2,1,0:T(8,128)(2,1)S(1)}, u32[]{:S(2)}, u32[]{:S(2)}) collective-permute-start(bf16[2,384,256]{2,1,0:T(8,128)(2,1)S(1)} %shard_map.195.solved), channel_id=1, source_target_pairs={{510,0},{0,2},{2,4},{4,6},{6,8},{8,10},{10,12},{12,14},{14,16},{16... | collective-permute-start | bytes 1179656 | tf_op jit(solution)/shard_map/ppermute | solution.py:283
